TPU v7x, 32 devices: a whole 2x2x4 slice. The times are simulated.
32 devices in a mesh: groups: 1, gx: 8 (over y, x, core), gy: 4 (over z).
Axes of the slice: x: 2, y: 2, z: 4, core: 2. Of those that a mesh axis runs over, the one named last changes fastest.
Arguments:
- tokens: bfloat16 [256, 8192], P(('groups', 'gx'), 'gy'), may hold values from -6 to 6
- w_gate: bfloat16 [8192, 64, 128], P('gy', 'gx'), may hold values from -0.0625 to 0.0625
- w_x: bfloat16 [8192, 64, 128], P('gy', 'gx'), may hold values from -0.0625 to 0.0625
- w_bc: bfloat16 [8192, 256], P('gy'), may hold values from -0.005859375 to 0.005859375
- w_dt: bfloat16 [8192, 64], P('gy', 'gx'), may hold values from -0.0625 to 0.0625
- conv_x_w: float32 [4, 64, 128], P(None, 'gx', 'gy'), may hold values from -3 to 3
- conv_bc_w: float32 [4, 256], replicated, may hold values from -3 to 3
- conv_x_state: float32 [3, 64, 128], P(None, ('groups', 'gx'), 'gy'), may hold values from -6 to 6
- conv_bc_state: float32 [3, 256], P(None, 'groups'), may hold values from -0.6 to 0.6
- dt_bias: float32 [64], P('gx'), may hold values from -1 to 1
- decay_rate: float32 [64], P('gx'), may hold values from 0.0003 to 0.1
- skip_d: float32 [64], P('gx'), may hold values from 0.5 to 1.5
- state_in: float32 [64, 128, 128], P(('groups', 'gx'), 'gy'), may hold values from -18 to 18
- norm_gain: float32 [64, 128], P('gx'), may hold values from 0.5 to 1.5
- w_out: bfloat16 [64, 128, 8192], P('gx', None, 'gy'), may hold values from -0.0625 to 0.0625
Outputs:
- mixed_out: bfloat16 [256, 8192], P(('groups', 'gx'), 'gy')
- state_out: float32 [64, 128, 128], P(('groups', 'gx'), 'gy')
All inputs are finite; a program needn't handle non-finite values.
Results may differ from a plain program's by a relative error of at most 0.02.
Values may be sent and summed in bfloat16 or wider, within the bound.
A program may use at most 64 MiB of HBM per device.

v0:
```python
import jax
import jax.numpy as jnp
from jax import lax
from jax.sharding import PartitionSpec as P

SSD_BLOCK = 256


def conv_silu(pre, carried, taps):
    padded = jnp.concatenate([carried, pre], axis=0)
    length = pre.shape[0]
    acc = jnp.zeros(pre.shape, jnp.float32)
    for index in range(taps.shape[0]):
        acc = acc + taps[index] * padded[index : index + length]
    return jax.nn.silu(acc)


def ssd_blocks(values, b_mat, c_mat, delta, log_decay, state, block):
    total, heads, width = values.shape
    count = total // block
    states = b_mat.shape[1]
    lower = jnp.arange(block)[:, None] >= jnp.arange(block)[None, :]
    high = lax.Precision.HIGHEST

    def advance(carry, inputs):
        vals, bm, cm, dl, ld = inputs
        cum = jnp.cumsum(ld, axis=0)
        scores = jnp.dot(cm, bm.T, precision=high)
        gap = cum.T[:, :, None] - cum.T[:, None, :]
        decay = jnp.exp(jnp.where(lower[None], gap, -jnp.inf))
        weights = decay * scores[None]
        scaled = vals * dl[:, :, None]
        inner = jnp.einsum("hts,shp->thp", weights, scaled, precision=high)
        carried = jnp.exp(cum)[:, :, None] * jnp.einsum("tn,hpn->thp", cm, carry, precision=high)
        tail = jnp.exp(cum[-1][None, :] - cum)
        update = jnp.einsum("sh,shp,sn->hpn", tail, scaled, bm, precision=high)
        new_state = jnp.exp(cum[-1])[:, None, None] * carry + update
        return (new_state, inner + carried)

    inputs = (
        values.reshape(count, block, heads, width),
        b_mat.reshape(count, block, states),
        c_mat.reshape(count, block, states),
        delta.reshape(count, block, heads),
        log_decay.reshape(count, block, heads),
    )
    final, outputs = lax.scan(advance, state, inputs)
    return (outputs.reshape(total, heads, width), final)


def per_device(
    tokens,
    w_gate,
    w_x,
    w_bc,
    w_dt,
    conv_x_w,
    conv_bc_w,
    conv_x_state,
    conv_bc_state,
    dt_bias,
    decay_rate,
    skip_d,
    state_in,
    norm_gain,
    w_out,
):
    d_rows, heads_here, head_width = w_gate.shape
    inner_here = heads_here * head_width
    states_two = w_bc.shape[1]
    merged = jnp.concatenate(
        [w_gate.reshape(d_rows, inner_here), w_x.reshape(d_rows, inner_here), w_bc, w_dt], axis=1
    )
    projected = jnp.dot(
        lax.all_gather(tokens, "gx", axis=0, tiled=True), merged, preferred_element_type=jnp.float32
    )
    total = projected.shape[0]
    paired = projected[:, : 2 * inner_here].reshape(total, 2, heads_here, head_width)
    channels = lax.psum_scatter(
        paired.astype(jnp.bfloat16), "gy", scatter_dimension=3, tiled=True
    ).astype(jnp.float32)
    shared = lax.psum(projected[:, 2 * inner_here :].astype(jnp.bfloat16), "gy").astype(jnp.float32)
    gate_pre = channels[:, 0]
    x_pre = channels[:, 1]
    values = conv_silu(x_pre, conv_x_state, conv_x_w)
    bc_conv = conv_silu(shared[:, :states_two], conv_bc_state, conv_bc_w)
    half_states = states_two // 2
    b_mat = bc_conv[:, :half_states]
    c_mat = bc_conv[:, half_states:]
    delta = jax.nn.softplus(shared[:, states_two:] + dt_bias)
    log_decay = -delta * decay_rate
    ssm, state_out = ssd_blocks(values, b_mat, c_mat, delta, log_decay, state_in, SSD_BLOCK)
    ssm = ssm + skip_d[None, :, None] * values
    gated = ssm * jax.nn.silu(gate_pre)
    full_width = norm_gain.shape[1]
    whole = lax.all_gather(gated.astype(jnp.bfloat16), "gy", axis=2, tiled=True).astype(gated.dtype)
    square_mean = jnp.mean(whole * whole, axis=2, keepdims=True)
    normed = (whole * lax.rsqrt(square_mean + 1e-05) * norm_gain).astype(jnp.bfloat16)
    out_cols = w_out.shape[2]
    flat = normed.reshape(total, heads_here * full_width)
    w_flat = w_out.reshape(heads_here * full_width, out_cols)
    summed = lax.psum_scatter(
        jnp.dot(flat, w_flat, preferred_element_type=jnp.float32).astype(jnp.bfloat16),
        "gx",
        scatter_dimension=0,
        tiled=True,
    )
    return (summed, state_out)


def solution(mesh):
    in_specs = (
        P(("groups", "gx"), "gy"),
        P("gy", "gx", None),
        P("gy", "gx", None),
        P("gy", None),
        P("gy", "gx"),
        P(None, "gx", "gy"),
        P(),
        P(None, ("groups", "gx"), "gy"),
        P(None, "groups"),
        P("gx"),
        P("gx"),
        P("gx"),
        P(("groups", "gx"), "gy", None),
        P("gx", None),
        P("gx", None, "gy"),
    )
    out_specs = (P(("groups", "gx"), "gy"), P(("groups", "gx"), "gy", None))
    return jax.shard_map(
        per_device, mesh=mesh, in_specs=in_specs, out_specs=out_specs, check_vma=False
    )
```

profile of v0, /device:TPU:0, one launch (start us, length us, event | category | flops | bytes accessed | tf_op | source)
XLA Modules:
  0.0 176.8 jit_solution(11189340785434748447)
XLA Ops:
  7.2 0.7 all-gather.2.cloned.1.call-update
  7.9 1.0 copy.33
  9.0 8.7 %copy_bitcast_fusion = (bf16[2048,1024]{1,0:T(8,128)(2,1)}, bf16[2048,1024]{1,0:T(8,128)(2,1)}) fusion(bf16[256,8,8,128]{3,2,1,0:T(8,128)(2,1)} %bitcast.53, bf16[256,8,8,128]{3,2,1,0:T(8,128)(2,1)} %bitcast.54), kind=kLoop, calls=%fused_computation.8 | loop fusion | bytes 16777216 | tf_op jit(solution)/shard_map/reshape | solution.py:72
  17.7 18.4 %all-gather.2.cloned.1.call-done = bf16[256,2048]{1,0:T(8,128)(2,1)} async-done(((bf16[32,2048]{1,0:T(8,128)(2,1)}), bf16[256,2048]{1,0:T(8,128)(2,1)}) %all-gather.2.cloned.1.call-update) | async-done | bytes 1048592 | tf_op jit(solution)/shard_map/all_gather | solution.py:75
  36.1 11.7 %fusion.11 = bf16[256,2312]{0,1:T(8,128)(2,1)S(1)} fusion(bf16[256,2048]{1,0:T(8,128)(2,1)} %all-gather.2.cloned.1.call-done, bf16[2048,8]{1,0:T(8,128)(2,1)S(1)} %copy.33, bf16[2048,256]{1,0:T(8,128)(2,1)S(1)} %copy-done.8, bf16[2048,1024]{1,0:T(8,128)(2,1)} %get-tuple-element.41, bf16[2048,1024]{1,0:T(8,128)(2,1)} %get-tuple-element.42), kind=kOutput, calls=%fused_computation.11 | convolution fusion | flops 2462779392 | bytes 11702272 | tf_op jit(solution)/shard_map/dot_general | solution.py:74
  47.9 0.7 slice.110
  48.6 1.0 slice.104
  49.7 0.0 reduce-scatter.5.cloned.1.call-start
  49.7 0.1 copy.34
  49.9 0.1 copy.35
  50.1 33.0 %all-reduce.2.cloned.1.call-done = bf16[256,264]{0,1:T(8,128)(2,1)} async-done(((bf16[256,264]{0,1:T(8,128)(2,1)}), bf16[256,264]{0,1:T(8,128)(2,1)}) %all-reduce.2.cloned.1.call-update) | async-done | bytes 135184 | tf_op jit(solution)/shard_map/psum | solution.py:82
  83.1 0.9 convert_element_type.25
  84.1 0.1 multiply_bitcast_fusion
  84.2 0.6 reduce-window.6
  84.7 0.2 slice_reduce_fusion
  84.9 0.9 slice.113
  85.9 0.1 add_bitcast_fusion.1
  85.9 0.1 fusion.69
  86.0 0.5 divide_multiply_fusion
  86.5 0.4 fusion.63
  87.0 25.8 %reduce-scatter.3.cloned.1.call-done = bf16[256,2,8,32]{0,3,2,1:T(8,128)(2,1)} async-done(((bf16[256,2,8,128]{0,3,2,1:T(8,128)(2,1)}), bf16[256,2,8,32]{0,3,2,1:T(8,128)(2,1)}) %reduce-scatter.3.cloned.1.call-update) | async-done | bytes 262160 | tf_op jit(solution)/shard_map/reduce_scatter | solution.py:79
  112.8 1.1 convert_element_type.24
  113.9 0.5 divide_multiply_fusion.1
  114.4 2.3 %fusion.23 = f32[256,8,32]{0,2,1:T(8,128)S(1)} fusion(f32[256,256]{1,0:T(8,128)S(1)} %fusion.63, f32[8,256]{1,0:T(8,128)S(1)} %add_bitcast_fusion.1, pred[256,256]{1,0:T(8,128)(4,1)S(1)} %iota_compare_fusion, f32[256,8,32]{0,2,1:T(8,128)S(1)} %divide_multiply_fusion.1, f32[256,8]{0,1:T(8,128)S(1)} %get-tuple-element.23), kind=kOutput, calls=%fused_computation.25 | convolution fusion | flops 202964992 | bytes 868352 | tf_op jit(solution)/shard_map/while/body/eval_jaxpr/hts,shp->thp/dot_general | solution.py:33
  116.7 0.4 fusion.26
  117.1 16.0 %all_gather.7 = bf16[256,8,128]{0,2,1:T(8,128)(2,1)S(1)} all-gather(bf16[256,8,32]{0,2,1:T(8,128)(2,1)S(1)} %fusion.26), channel_id=1, replica_groups=mesh['groups'=1,'gx'=8,'gy'=4] {'gy'}, dimensions={2}, use_global_device_ids=true | all-gather | bytes 655360 | tf_op jit(solution)/shard_map/all_gather | solution.py:96
  133.2 0.1 fusion.27
  133.3 2.4 %fusion.14 = bf16[256,2048]{1,0:T(8,128)(2,1)} fusion(bf16[8,128,2048]{2,1,0:T(8,128)(2,1)S(1)} %copy-done.7, bf16[256,8,128]{0,2,1:T(8,128)(2,1)S(1)} %all_gather.7, f32[8,128]{1,0:T(8,128)S(1)} %copy-done.9, f32[256,8]{0,1:T(8,128)S(1)} %add_rsqrt_fusion), kind=kOutput, calls=%fused_computation.13 | convolution fusion | flops 1075314688 | bytes 5779456 | tf_op jit(solution)/shard_map/dot_general | solution.py:103
  135.7 0.2 slice_reduce_fusion.1
  135.9 0.1 subtract_exponential_fusion
  136.0 1.0 convolution_add_fusion
  137.0 33.2 %reduce-scatter.5.cloned.1.call-done = bf16[32,2048]{1,0:T(8,128)(2,1)} async-done(((bf16[256,2048]{1,0:T(8,128)(2,1)}), bf16[32,2048]{1,0:T(8,128)(2,1)}) %reduce-scatter.5.cloned.1.call-update) | async-done | bytes 131088 | tf_op jit(solution)/shard_map/reduce_scatter | solution.py:102
  (36 shorter events, 0.3 us)
Async XLA Ops:
  7.2 28.9 %all-gather.2.cloned.1.call-start = ((), (), s32[]{:S(2)}) async-start(), calls=%async_computation.2 | async-start | bytes 1179648 | tf_op jit(solution)/shard_map/all_gather | solution.py:75
  7.9 75.2 %all-reduce.2.cloned.1.call-start = ((), (), s32[]{:S(2)}) async-start(), calls=%async_computation.4 | async-start | bytes 270336 | tf_op jit(solution)/shard_map/psum | solution.py:82
  9.0 27.1 %copy-start.8 = (bf16[2048,256]{1,0:T(8,128)(2,1)S(1)}, bf16[2048,256]{1,0:T(8,128)(2,1)}, u32[]{:S(2)}) copy-start(bf16[2048,256]{1,0:T(8,128)(2,1)} %param.18) | copy-start | bytes 3145732
  36.1 13.6 %copy-start.2 = (f32[3,8,32]{2,1,0:T(8,128)S(1)}, f32[3,8,32]{2,1,0:T(8,128)}, u32[]{:S(2)}) copy-start(f32[3,8,32]{2,1,0:T(8,128)} %param.22) | copy-start | bytes 9220
  36.1 13.7 %copy-start.3 = (f32[3,256]{1,0:T(4,128)S(1)}, f32[3,256]{1,0:T(4,128)}, u32[]{:S(2)}) copy-start(f32[3,256]{1,0:T(4,128)} %param.23) | copy-start | bytes 9220
  36.1 13.9 %copy-start.4 = (f32[4,256]{1,0:T(4,128)S(1)}, f32[4,256]{1,0:T(4,128)}, u32[]{:S(2)}) copy-start(f32[4,256]{1,0:T(4,128)} %param.21) | copy-start | bytes 12292
  36.1 13.9 %copy-start.1 = (f32[4,8,32]{2,1,0:T(8,128)S(1)}, f32[4,8,32]{2,1,0:T(8,128)}, u32[]{:S(2)}) copy-start(f32[4,8,32]{2,1,0:T(8,128)} %param.20) | copy-start | bytes 12292
  47.9 36.2 %copy-start.5 = (f32[8]{0:T(128)S(1)}, f32[8]{0:T(128)}, u32[]{:S(2)}) copy-start(f32[8]{0:T(128)} %param.25) | copy-start | bytes 100
  47.9 36.2 %copy-start.6 = (f32[8]{0:T(128)S(1)}, f32[8]{0:T(128)}, u32[]{:S(2)}) copy-start(f32[8]{0:T(128)} %param.24) | copy-start | bytes 100
  48.6 64.2 %reduce-scatter.3.cloned.1.call-start = ((), (), s32[]{:S(2)}) async-start(), calls=%async_computation.3 | async-start | bytes 1310720 | tf_op jit(solution)/shard_map/reduce_scatter | solution.py:79
  49.6 67.1 %copy-start = (f32[8,32,128]{2,1,0:T(8,128)S(1)}, f32[8,32,128]{2,1,0:T(8,128)}, u32[]{:S(2)}) copy-start(f32[8,32,128]{2,1,0:T(8,128)} %param.27) | copy-start | bytes 393220
  49.6 67.1 %copy-start.10 = (f32[8]{0:T(128)S(1)}, f32[8]{0:T(128)}, u32[]{:S(2)}) copy-start(f32[8]{0:T(128)} %param.26) | copy-start | bytes 100
  49.7 120.6 %reduce-scatter.5.cloned.1.call-start = ((), (), s32[]{:S(2)}) async-start(), calls=%async_computation.5 | async-start | bytes 1179648 | tf_op jit(solution)/shard_map/reduce_scatter | solution.py:102
  86.5 46.8 %copy-start.9 = (f32[8,128]{1,0:T(8,128)S(1)}, f32[8,128]{1,0:T(8,128)}, u32[]{:S(2)}) copy-start(f32[8,128]{1,0:T(8,128)} %param.28) | copy-start | bytes 12292
  112.7 20.6 %copy-start.7 = (bf16[8,128,2048]{2,1,0:T(8,128)(2,1)S(1)}, bf16[8,128,2048]{2,1,0:T(8,128)(2,1)}, u32[]{:S(2)}) copy-start(bf16[8,128,2048]{2,1,0:T(8,128)(2,1)} %param.29) | copy-start | bytes 12582916
Sparse Core Ops, SparseCore 0:
  9.9 26.1 all-gather.1
  48.7 34.3 all-reduce.1
  85.5 27.1 reduce-scatter.2
  135.8 34.3 reduce-scatter.4
where the time goes:
time: 177 us
  waiting for transfers between devices  111 us (63%)
  matrix products  18.2 us (10%)
  blocking collectives  16 us (9%)
  between operations  14 us (8%)
  local copies, waits for them, and re-layouts  13.1 us (7%)
  other arithmetic  4.14 us (2%)
    reduce_scatter x1, waiting for transfers between devices, per_device(): lax.psum_scatter(jnp.dot(flat, w_flat, preferred_element_type=jnp.float32...  33.2 us
    psum x1, waiting for transfers between devices, per_device(): lax.psum(projected[:, 2 * inner_here:].astype(jnp.bfloat16), 'gy')  33 us
    reduce_scatter x1, waiting for transfers between devices, per_device(): lax.psum_scatter(paired.astype(jnp.bfloat16), 'gy', scatter_dimension=3,...  25.8 us
    all_gather x1, waiting for transfers between devices, per_device(): lax.all_gather(tokens, 'gx', axis=0, tiled=True)  18.4 us
    all_gather x1, blocking collectives, per_device(): lax.all_gather(gated.astype(jnp.bfloat16), 'gy', axis=2, tiled=True)  16 us
    dot_general x1, matrix products, per_device(): jnp.dot(lax.all_gather(tokens, 'gx', axis=0, tiled=True), merged, preferr...  11.7 us
    reshape x1, local copies, waits for them, and re-layouts, per_device(): w_x.reshape(d_rows, inner_here)  8.7 us
  transfers between devices with their start and end apart: 4, of which 4 were waited for; matrix products, arithmetic and copies ran while one was open for 9% of the time, Pallas kernels for 0%

commit v1 on v0

--- a/solution.py
+++ b/solution.py
@@ -1,6 +1,10 @@
+import functools
+
 import jax
 import jax.numpy as jnp
 from jax import lax
+from jax.experimental import pallas as pl
+from jax.experimental.pallas import tpu as pltpu
 from jax.sharding import PartitionSpec as P
 
 SSD_BLOCK = 256
@@ -46,6 +50,197 @@
     )
     final, outputs = lax.scan(advance, state, inputs)
     return (outputs.reshape(total, heads, width), final)
+
+
+VM = pl.BlockSpec(memory_space=pltpu.VMEM)
+HBM = pl.BlockSpec(memory_space=pl.ANY)
+MESH = pl.DeviceIdType.MESH
+TILE = 256
+
+
+def greet(n_gx, n_gy):
+    barrier = pltpu.get_barrier_semaphore()
+    for axis, count in (("gx", n_gx), ("gy", n_gy)):
+        me = lax.axis_index(axis)
+        for step in range(1, count):
+            peer = lax.rem(me + step, count)
+            pl.semaphore_signal(barrier, inc=1, device_id={axis: peer}, device_id_type=MESH)
+    pl.semaphore_wait(barrier, n_gx + n_gy - 2)
+
+
+def remote(src, dst, send, recv, axis, peer):
+    return pltpu.make_async_remote_copy(
+        src_ref=src,
+        dst_ref=dst,
+        send_sem=send,
+        recv_sem=recv,
+        device_id={axis: peer},
+        device_id_type=MESH,
+    )
+
+
+def project_kernel(
+    n_gx, n_gy, heads, width,
+    tok_ref, wg_ref, wx_ref, wbc_ref, wdt_ref,
+    chan_ref, bc_ref, dt_ref,
+    full, w, wbc, part, snd, rcv, bc_rcv, bc_full, dt_rcv,
+    load_sem, gx_send, gx_recv, gy_send, gy_recv,
+):
+    gx, gy = lax.axis_index("gx"), lax.axis_index("gy")
+    rows = tok_ref.shape[0]
+    inner = heads * width
+    local = width // n_gy
+    loads = [
+        pltpu.make_async_copy(wbc_ref, wbc, load_sem.at[0]),
+        pltpu.make_async_copy(wg_ref, w.at[:, pl.ds(0, inner)], load_sem.at[1]),
+        pltpu.make_async_copy(wx_ref, w.at[:, pl.ds(inner, inner)], load_sem.at[2]),
+    ]
+    for load in loads:
+        load.start()
+    greet(n_gx, n_gy)
+    mine = pl.ds(pl.multiple_of(gx * rows, rows), rows)
+    gathers = []
+    for step in range(1, n_gx):
+        peer = lax.rem(gx + step, n_gx)
+        copy = remote(
+            tok_ref, full.at[mine], gx_send.at[0, step], gx_recv.at[0, step], "gx", peer
+        )
+        copy.start()
+        gathers.append(copy)
+    full[mine] = tok_ref[...]
+    loads[0].wait()
+    bc_rcv[0] = jnp.dot(tok_ref[...], wbc[...], preferred_element_type=jnp.float32)
+    bc_sums = []
+    for step in range(1, n_gy):
+        peer = lax.rem(gy + step, n_gy)
+        copy = remote(
+            bc_rcv.at[0], bc_rcv.at[step], gy_send.at[0, step], gy_recv.at[0, step], "gy", peer
+        )
+        copy.start()
+        bc_sums.append(copy)
+    for copy in bc_sums:
+        copy.wait()
+    bc_sum = bc_rcv[0]
+    for step in range(1, n_gy):
+        bc_sum = bc_sum + bc_rcv[step]
+    bc_full[mine] = bc_sum
+    bc_gathers = []
+    for step in range(1, n_gx):
+        peer = lax.rem(gx + step, n_gx)
+        copy = remote(
+            bc_full.at[mine], bc_full.at[mine], gx_send.at[1, step], gx_recv.at[1, step], "gx", peer
+        )
+        copy.start()
+        bc_gathers.append(copy)
+    for copy in gathers:
+        copy.wait()
+    dt_rcv[0] = lax.dot_general(
+        wdt_ref[...], full[...], (((1,), (1,)), ((), ())), preferred_element_type=jnp.float32
+    )
+    dt_sums = []
+    for step in range(1, n_gy):
+        peer = lax.rem(gy + step, n_gy)
+        copy = remote(
+            dt_rcv.at[0], dt_rcv.at[step], gy_send.at[1, step], gy_recv.at[1, step], "gy", peer
+        )
+        copy.start()
+        dt_sums.append(copy)
+    loads[1].wait()
+    loads[2].wait()
+
+    def tile(index, carry):
+        cols = pl.ds(pl.multiple_of(index * TILE, TILE), TILE)
+        part[:, cols] = jnp.dot(full[...], w[:, cols], preferred_element_type=jnp.float32)
+        return carry
+
+    lax.fori_loop(0, 2 * inner // TILE, tile, 0)
+    for owner in range(n_gy):
+        pieces = [
+            part[:, head * width + owner * local : head * width + (owner + 1) * local]
+            for head in range(2 * heads)
+        ]
+        snd[owner] = jnp.concatenate(pieces, axis=1).astype(jnp.bfloat16)
+    sums = []
+    for step in range(1, n_gy):
+        peer = lax.rem(gy + step, n_gy)
+        copy = remote(
+            snd.at[peer], rcv.at[step], gy_send.at[2, step], gy_recv.at[2, step], "gy", peer
+        )
+        copy.start()
+        sums.append(copy)
+    for copy in bc_gathers:
+        copy.wait()
+    bc_ref[...] = bc_full[...]
+    for copy in dt_sums:
+        copy.wait()
+    dt_sum = dt_rcv[0]
+    for step in range(1, n_gy):
+        dt_sum = dt_sum + dt_rcv[step]
+    dt_ref[...] = dt_sum
+    for copy in sums:
+        copy.wait()
+    total = snd[gy].astype(jnp.float32)
+    for step in range(1, n_gy):
+        total = total + rcv[step].astype(jnp.float32)
+    chan_ref[...] = total
+
+
+def out_kernel(
+    n_gx, n_gy, heads, width,
+    gated_ref, gain_ref, w_ref, out_ref,
+    whole, normed, w, prod, rcv,
+    load_sem, gy_sem, gx_sem,
+):
+    gx, gy = lax.axis_index("gx"), lax.axis_index("gy")
+    rows, out_cols = out_ref.shape
+    local = width // n_gy
+    load = pltpu.make_async_copy(w_ref, w, load_sem.at[0])
+    load.start()
+    greet(n_gx, n_gy)
+    copies = []
+    for step in range(1, n_gy):
+        peer = lax.rem(gy + step, n_gy)
+        copy = remote(
+            gated_ref, whole.at[gy], gy_sem.at[0, step], gy_sem.at[1, step], "gy", peer
+        )
+        copy.start()
+        copies.append(copy)
+    whole[gy] = gated_ref[...]
+    for copy in copies:
+        copy.wait()
+    blocks = [whole[owner].astype(jnp.float32) for owner in range(n_gy)]
+    for head in range(heads):
+        row = jnp.concatenate(
+            [block[:, head * local : (head + 1) * local] for block in blocks], axis=1
+        )
+        mean = jnp.mean(row * row, axis=1, keepdims=True)
+        normed[:, head * width : (head + 1) * width] = (
+            row * lax.rsqrt(mean + 1e-05) * gain_ref[head : head + 1, :]
+        ).astype(jnp.bfloat16)
+    load.wait()
+
+    def tile(index, carry):
+        cols = pl.ds(pl.multiple_of(index * TILE, TILE), TILE)
+        prod[:, cols] = jnp.dot(
+            normed[...], w[:, cols], preferred_element_type=jnp.float32
+        ).astype(jnp.bfloat16)
+        return carry
+
+    lax.fori_loop(0, out_cols // TILE, tile, 0)
+    copies = []
+    for step in range(1, n_gx):
+        peer = lax.rem(gx + step, n_gx)
+        theirs = pl.ds(pl.multiple_of(peer * rows, rows), rows)
+        copy = remote(
+            prod.at[theirs], rcv.at[step], gx_sem.at[0, step], gx_sem.at[1, step], "gx", peer
+        )
+        copy.start()
+        copies.append(copy)
+    total = prod[pl.ds(pl.multiple_of(gx * rows, rows), rows)].astype(jnp.float32)
+    for step in range(1, n_gx):
+        copies[step - 1].wait()
+        total = total + rcv[step].astype(jnp.float32)
+    out_ref[...] = total.astype(jnp.bfloat16)
 
 
 def per_device(
@@ -65,46 +260,84 @@
     norm_gain,
     w_out,
 ):
+    n_gx, n_gy = lax.axis_size("gx"), lax.axis_size("gy")
     d_rows, heads_here, head_width = w_gate.shape
     inner_here = heads_here * head_width
     states_two = w_bc.shape[1]
-    merged = jnp.concatenate(
-        [w_gate.reshape(d_rows, inner_here), w_x.reshape(d_rows, inner_here), w_bc, w_dt], axis=1
-    )
-    projected = jnp.dot(
-        lax.all_gather(tokens, "gx", axis=0, tiled=True), merged, preferred_element_type=jnp.float32
-    )
-    total = projected.shape[0]
-    paired = projected[:, : 2 * inner_here].reshape(total, 2, heads_here, head_width)
-    channels = lax.psum_scatter(
-        paired.astype(jnp.bfloat16), "gy", scatter_dimension=3, tiled=True
-    ).astype(jnp.float32)
-    shared = lax.psum(projected[:, 2 * inner_here :].astype(jnp.bfloat16), "gy").astype(jnp.float32)
-    gate_pre = channels[:, 0]
-    x_pre = channels[:, 1]
-    values = conv_silu(x_pre, conv_x_state, conv_x_w)
-    bc_conv = conv_silu(shared[:, :states_two], conv_bc_state, conv_bc_w)
+    rows = tokens.shape[0]
+    total = rows * n_gx
+    local = head_width // n_gy
+    seg = heads_here * local
+    channels, bc_pre, dt_pre = pl.pallas_call(
+        functools.partial(project_kernel, n_gx, n_gy, heads_here, head_width),
+        out_shape=(
+            jax.ShapeDtypeStruct((total, 2 * seg), jnp.float32),
+            jax.ShapeDtypeStruct((total, states_two), jnp.float32),
+            jax.ShapeDtypeStruct((heads_here, total), jnp.float32),
+        ),
+        in_specs=[VM, HBM, HBM, HBM, VM],
+        out_specs=(VM, VM, VM),
+        scratch_shapes=[
+            pltpu.VMEM((total, d_rows), jnp.bfloat16),
+            pltpu.VMEM((d_rows, 2 * inner_here), jnp.bfloat16),
+            pltpu.VMEM((d_rows, states_two), jnp.bfloat16),
+            pltpu.VMEM((total, 2 * inner_here), jnp.float32),
+            pltpu.VMEM((n_gy, total, 2 * seg), jnp.bfloat16),
+            pltpu.VMEM((n_gy, total, 2 * seg), jnp.bfloat16),
+            pltpu.VMEM((n_gy, rows, states_two), jnp.float32),
+            pltpu.VMEM((total, states_two), jnp.float32),
+            pltpu.VMEM((n_gy, heads_here, total), jnp.float32),
+            pltpu.SemaphoreType.DMA((3,)),
+            pltpu.SemaphoreType.DMA((2, n_gx)),
+            pltpu.SemaphoreType.DMA((2, n_gx)),
+            pltpu.SemaphoreType.DMA((3, n_gy)),
+            pltpu.SemaphoreType.DMA((3, n_gy)),
+        ],
+        compiler_params=pltpu.CompilerParams(
+            collective_id=0, has_side_effects=True, vmem_limit_bytes=48 * 1024 * 1024
+        ),
+    )(
+        tokens,
+        w_gate.reshape(d_rows, inner_here),
+        w_x.reshape(d_rows, inner_here),
+        w_bc,
+        w_dt.T,
+    )
+    gate_pre = channels[:, :seg]
+    taps = conv_x_w.shape[0]
+    flat_values = conv_silu(
+        channels[:, seg:], conv_x_state.reshape(taps - 1, seg), conv_x_w.reshape(taps, seg)
+    )
+    values = flat_values.reshape(total, heads_here, local)
+    bc_conv = conv_silu(bc_pre, conv_bc_state, conv_bc_w)
     half_states = states_two // 2
     b_mat = bc_conv[:, :half_states]
     c_mat = bc_conv[:, half_states:]
-    delta = jax.nn.softplus(shared[:, states_two:] + dt_bias)
+    delta = jax.nn.softplus(dt_pre.T + dt_bias)
     log_decay = -delta * decay_rate
     ssm, state_out = ssd_blocks(values, b_mat, c_mat, delta, log_decay, state_in, SSD_BLOCK)
     ssm = ssm + skip_d[None, :, None] * values
-    gated = ssm * jax.nn.silu(gate_pre)
-    full_width = norm_gain.shape[1]
-    whole = lax.all_gather(gated.astype(jnp.bfloat16), "gy", axis=2, tiled=True).astype(gated.dtype)
-    square_mean = jnp.mean(whole * whole, axis=2, keepdims=True)
-    normed = (whole * lax.rsqrt(square_mean + 1e-05) * norm_gain).astype(jnp.bfloat16)
+    gated = (ssm.reshape(total, seg) * jax.nn.silu(gate_pre)).astype(jnp.bfloat16)
     out_cols = w_out.shape[2]
-    flat = normed.reshape(total, heads_here * full_width)
-    w_flat = w_out.reshape(heads_here * full_width, out_cols)
-    summed = lax.psum_scatter(
-        jnp.dot(flat, w_flat, preferred_element_type=jnp.float32).astype(jnp.bfloat16),
-        "gx",
-        scatter_dimension=0,
-        tiled=True,
-    )
+    summed = pl.pallas_call(
+        functools.partial(out_kernel, n_gx, n_gy, heads_here, head_width),
+        out_shape=jax.ShapeDtypeStruct((rows, out_cols), jnp.bfloat16),
+        in_specs=[VM, VM, HBM],
+        out_specs=VM,
+        scratch_shapes=[
+            pltpu.VMEM((n_gy, total, seg), jnp.bfloat16),
+            pltpu.VMEM((total, inner_here), jnp.bfloat16),
+            pltpu.VMEM((inner_here, out_cols), jnp.bfloat16),
+            pltpu.VMEM((total, out_cols), jnp.bfloat16),
+            pltpu.VMEM((n_gx, rows, out_cols), jnp.bfloat16),
+            pltpu.SemaphoreType.DMA((1,)),
+            pltpu.SemaphoreType.DMA((2, n_gy)),
+            pltpu.SemaphoreType.DMA((2, n_gx)),
+        ],
+        compiler_params=pltpu.CompilerParams(
+            collective_id=1, has_side_effects=True, vmem_limit_bytes=48 * 1024 * 1024
+        ),
+    )(gated, norm_gain, w_out.reshape(inner_here, out_cols))
     return (summed, state_out)
 
 

time: 177 us -> 98.3 us (0.56)
  the two profiles are of different devices: /device:TPU:0 before, /device:TPU:9 now
where the time goes in v1:
time: 98.3 us; the launch traced here: 98.1 us
  Pallas kernels  79.4 us (81%)
  local copies, waits for them, and re-layouts  12.2 us (12%)
  matrix products  4.09 us (4%)
  other arithmetic  1.5 us (2%)
    pallas_call x1, Pallas kernels, per_device(): pl.pallas_call(functools.partial(project_kernel, n_gx, n_gy, heads_here,...  47.2 us
    pallas_call x1, Pallas kernels, per_device(): pl.pallas_call(functools.partial(out_kernel, n_gx, n_gy, heads_here, head...  32.2 us
    reshape x1, local copies, waits for them, and re-layouts, per_device(): w_x.reshape(d_rows, inner_here)  8.11 us
    unnamed x27, local copies, waits for them, and re-layouts  2.91 us
    dot_general x1, matrix products, advance(): inner = jnp.einsum('hts,shp->thp', weights, scaled, precision=high)  2.3 us

profile of v1, /device:TPU:9, one launch (start us, length us, event | category | flops | bytes accessed | tf_op | source)
XLA Modules:
  0.0 98.1 jit_solution(12299784653128663361)
XLA Ops:
  0.7 8.1 %copy_bitcast_fusion = (bf16[2048,1024]{1,0:T(8,128)(2,1)}, bf16[2048,1024]{1,0:T(8,128)(2,1)S(1)}) fusion(bf16[256,8,8,128]{3,2,1,0:T(8,128)(2,1)} %bitcast.49, bf16[256,8,8,128]{3,2,1,0:T(8,128)(2,1)} %bitcast.50), kind=kLoop, calls=%fused_computation | loop fusion | bytes 16777216 | tf_op jit(solution)/shard_map/reshape | solution.py:302
  8.8 0.0 copy-start.11
  8.8 0.0 copy-start.6
  8.8 0.0 copy-start.8
  8.9 47.2 %shard_map.158 = (f32[256,512]{1,0:T(8,128)S(1)}, f32[256,256]{1,0:T(8,128)S(1)}, f32[8,256]{1,0:T(8,128)S(1)}) custom-call(bf16[32,2048]{1,0:T(8,128)(2,1)S(1)} %copy-done.2, bf16[2048,1024]{1,0:T(8,128)(2,1)S(1)} %get-tuple-element.46.wg_ref, bf16[2048,1024]{1,0:T(8,128)(2,1)} %get-tuple-element.45.wx_ref, bf16[2048,256]{1,0:T(8,128)(2,1)S(1)} %copy-done.1, ...), custom_call_target="tpu_custom_call" | custom-call | tf_op jit(solution)/shard_map/pallas_call | solution.py:271
  56.1 0.1 fusion.45
  56.2 0.6 reduce-window.6
  56.8 0.2 slice_reduce_fusion
  57.0 0.1 fusion.51
  57.0 0.2 slice_reduce_fusion.1
  57.2 0.1 subtract_exponential_fusion
  57.4 0.1 mul.163
  57.4 0.1 mul.166
  57.5 0.1 mul.169
  57.6 0.1 mul.172
  57.7 0.1 reshape.101
  57.8 0.2 divide_multiply_fusion.1
  57.9 0.1 copy.25
  58.1 0.2 divide_multiply_fusion
  58.3 0.1 compare_select_fusion.1
  58.4 1.0 %convolution_add_fusion = f32[8,32,128]{2,1,0:T(8,128)} fusion(f32[256,8,32]{0,2,1:T(8,128)S(1)} %bitcast.52, f32[256,8]{0,1:T(8,128)S(1)} %subtract_exponential_fusion, f32[8,32,128]{2,1,0:T(8,128)S(1)} %copy-done.5, f32[256,8]{0,1:T(8,128)S(1)} %compare_select_fusion.1, f32[256,256]{1,0:T(8,128)S(1)} %divide_multiply_fusion, f32[8]{0:T(128)S(1)} %exp.44), kind=kOutput, calls=%fused_computation.10 | convolution fusion | flops 100859904 | bytes 672256 | tf_op jit(solution)/shard_map/while/body/eval_jaxpr/sh,shp,sn->hpn/dot_general | solution.py:40
  59.4 0.4 fusion.39
  59.8 0.1 add_bitcast_fusion.1
  59.9 2.3 %fusion.6 = f32[256,8,32]{0,2,1:T(8,128)S(1)} fusion(f32[256,256]{1,0:T(8,128)S(1)} %fusion.39, f32[8,256]{1,0:T(8,128)S(1)} %add_bitcast_fusion.1, pred[256,256]{1,0:T(8,128)(4,1)S(1)} %iota_compare_fusion, f32[256,8,32]{0,2,1:T(8,128)S(1)} %bitcast.53, f32[256,8]{0,1:T(8,128)S(1)} %compare_select_fusion.1), kind=kOutput, calls=%fused_computation.9 | convolution fusion | flops 202964992 | bytes 868352 | tf_op jit(solution)/shard_map/while/body/eval_jaxpr/hts,shp->thp/dot_general | solution.py:37
  62.2 0.4 fusion.5
  62.6 0.1 copy.26
  62.8 0.1 mul.197
  62.8 0.1 mul.198
  62.9 0.1 multiply_convert_fusion.gated_ref
  63.0 2.2 %copy-done = bf16[8,128,2048]{2,1,0:T(8,128)(2,1)S(1)} copy-done((bf16[8,128,2048]{2,1,0:T(8,128)(2,1)S(1)}, bf16[8,128,2048]{2,1,0:T(8,128)(2,1)}, u32[]{:S(2)}) %copy-start) | copy-done | bytes 4194328
  65.2 32.2 %shard_map.159 = bf16[32,2048]{1,0:T(8,128)(2,1)S(1)} custom-call(bf16[256,256]{1,0:T(8,128)(2,1)S(1)} %multiply_convert_fusion.gated_ref, f32[8,128]{1,0:T(8,128)S(1)} %copy-done.4, bf16[1024,2048]{1,0:T(8,128)(2,1)S(1)} %bitcast.47), custom_call_target="tpu_custom_call" | custom-call | tf_op jit(solution)/shard_map/pallas_call | solution.py:322
  97.5 0.7 copy.32
  (29 shorter events, 0.2 us)
Async XLA Ops:
  0.6 8.1 %copy-start.1 = (bf16[2048,256]{1,0:T(8,128)(2,1)S(1)}, bf16[2048,256]{1,0:T(8,128)(2,1)}, u32[]{:S(2)}) copy-start(bf16[2048,256]{1,0:T(8,128)(2,1)} %wbc_ref.1) | copy-start | bytes 3145732
  0.6 8.1 %copy-start.2 = (bf16[32,2048]{1,0:T(8,128)(2,1)S(1)}, bf16[32,2048]{1,0:T(8,128)(2,1)}, u32[]{:S(2)}) copy-start(bf16[32,2048]{1,0:T(8,128)(2,1)} %tok_ref.1) | copy-start | bytes 393220
  0.7 8.1 %copy-start.3 = (bf16[2048,8]{0,1:T(8,128)(2,1)S(1)}, bf16[2048,8]{0,1:T(8,128)(2,1)}, u32[]{:S(2)}) copy-start(bf16[2048,8]{0,1:T(8,128)(2,1)} %param.19) | copy-start | bytes 98308
  8.8 47.3 %copy-start.10 = (f32[8]{0:T(128)S(1)}, f32[8]{0:T(128)}, u32[]{:S(2)}) copy-start(f32[8]{0:T(128)} %param.24) | copy-start | bytes 100
  8.8 47.3 %copy-start.11 = (f32[8]{0:T(128)S(1)}, f32[8]{0:T(128)}, u32[]{:S(2)}) copy-start(f32[8]{0:T(128)} %param.25) | copy-start | bytes 100
  8.8 48.5 %copy-start.6 = (f32[4,8,32]{2,1,0:T(8,128)S(1)}, f32[4,8,32]{2,1,0:T(8,128)}, u32[]{:S(2)}) copy-start(f32[4,8,32]{2,1,0:T(8,128)} %param.20) | copy-start | bytes 12292
  8.8 48.9 %copy-start.7 = (f32[3,8,32]{2,1,0:T(8,128)S(1)}, f32[3,8,32]{2,1,0:T(8,128)}, u32[]{:S(2)}) copy-start(f32[3,8,32]{2,1,0:T(8,128)} %param.22) | copy-start | bytes 9220
  8.8 49.3 %copy-start.9 = (f32[4,256]{1,0:T(4,128)S(1)}, f32[4,256]{1,0:T(4,128)}, u32[]{:S(2)}) copy-start(f32[4,256]{1,0:T(4,128)} %param.21) | copy-start | bytes 12292
  8.8 49.3 %copy-start.8 = (f32[3,256]{1,0:T(4,128)S(1)}, f32[3,256]{1,0:T(4,128)}, u32[]{:S(2)}) copy-start(f32[3,256]{1,0:T(4,128)} %param.23) | copy-start | bytes 9220
  8.9 49.5 %copy-start.5 = (f32[8,32,128]{2,1,0:T(8,128)S(1)}, f32[8,32,128]{2,1,0:T(8,128)}, u32[]{:S(2)}) copy-start(f32[8,32,128]{2,1,0:T(8,128)} %param.27) | copy-start | bytes 393220
  56.0 6.7 %copy-start.12 = (f32[8]{0:T(128)S(1)}, f32[8]{0:T(128)}, u32[]{:S(2)}) copy-start(f32[8]{0:T(128)} %param.26) | copy-start | bytes 100
  57.3 5.7 %copy-start.4 = (f32[8,128]{1,0:T(8,128)S(1)}, f32[8,128]{1,0:T(8,128)}, u32[]{:S(2)}) copy-start(f32[8,128]{1,0:T(8,128)} %gain_ref.1) | copy-start | bytes 12292
  63.0 2.2 %copy-start = (bf16[8,128,2048]{2,1,0:T(8,128)(2,1)S(1)}, bf16[8,128,2048]{2,1,0:T(8,128)(2,1)}, u32[]{:S(2)}) copy-start(bf16[8,128,2048]{2,1,0:T(8,128)(2,1)} %param.29) | copy-start | bytes 12582916

commit v2 on v1

--- a/solution.py
+++ b/solution.py
@@ -56,6 +56,9 @@
 HBM = pl.BlockSpec(memory_space=pl.ANY)
 MESH = pl.DeviceIdType.MESH
 TILE = 256
+DEPTH = 128
+LANES = 128
+CHUNKS = 2
 
 
 def greet(n_gx, n_gy):
@@ -83,30 +86,38 @@
     n_gx, n_gy, heads, width,
     tok_ref, wg_ref, wx_ref, wbc_ref, wdt_ref,
     chan_ref, bc_ref, dt_ref,
-    full, w, wbc, part, snd, rcv, bc_rcv, bc_full, dt_rcv,
-    load_sem, gx_send, gx_recv, gy_send, gy_recv,
+    full, raw, w, wbc, spread, part, snd, rcv, bc_rcv, bc_full, dt_rcv,
+    load_sem, gx_send, gx_recv, gy_send, gy_recv, sum_send, sum_recv,
 ):
     gx, gy = lax.axis_index("gx"), lax.axis_index("gy")
     rows = tok_ref.shape[0]
-    inner = heads * width
+    depth = wg_ref.shape[0]
     local = width // n_gy
+    core, chip, chips = gx % 2, gx // 2, n_gx // 2
+    sibling = gx + 1 - 2 * core
     loads = [
         pltpu.make_async_copy(wbc_ref, wbc, load_sem.at[0]),
-        pltpu.make_async_copy(wg_ref, w.at[:, pl.ds(0, inner)], load_sem.at[1]),
-        pltpu.make_async_copy(wx_ref, w.at[:, pl.ds(inner, inner)], load_sem.at[2]),
+        pltpu.make_async_copy(wg_ref, raw.at[0], load_sem.at[1]),
+        pltpu.make_async_copy(wx_ref, raw.at[1], load_sem.at[2]),
     ]
     for load in loads:
         load.start()
     greet(n_gx, n_gy)
-    mine = pl.ds(pl.multiple_of(gx * rows, rows), rows)
-    gathers = []
-    for step in range(1, n_gx):
-        peer = lax.rem(gx + step, n_gx)
+
+    def block(index):
+        return pl.ds(pl.multiple_of(index * rows, rows), rows)
+
+    mine = block(gx)
+    crossing = []
+    for step in range(1, chips):
+        peer = ((chip + step) % chips) * 2 + core
         copy = remote(
             tok_ref, full.at[mine], gx_send.at[0, step], gx_recv.at[0, step], "gx", peer
         )
         copy.start()
-        gathers.append(copy)
+        crossing.append(copy)
+    paired = [remote(tok_ref, full.at[mine], gx_send.at[0, 0], gx_recv.at[0, 0], "gx", sibling)]
+    paired[0].start()
     full[mine] = tok_ref[...]
     loads[0].wait()
     bc_rcv[0] = jnp.dot(tok_ref[...], wbc[...], preferred_element_type=jnp.float32)
@@ -118,6 +129,32 @@
         )
         copy.start()
         bc_sums.append(copy)
+
+    def flatten(which):
+        def body(index, carry):
+            start = pl.multiple_of(index * DEPTH, DEPTH)
+            chunk = raw[which, pl.ds(start, DEPTH)].astype(jnp.float32)
+            spread[...] = chunk.reshape(DEPTH * heads, width)
+            for head in range(heads):
+                column = (which * heads + head) * width
+                w[pl.ds(start, DEPTH), column : column + width] = spread[
+                    pl.ds(head, DEPTH, stride=heads), :
+                ].astype(jnp.bfloat16)
+            return carry
+
+        loads[1 + which].wait()
+        lax.fori_loop(0, depth // DEPTH, body, 0)
+
+    flatten(0)
+    for step in range(1, chips):
+        crossing[step - 1].wait()
+        came = block(((chip + chips - step) % chips) * 2 + core)
+        copy = remote(
+            full.at[came], full.at[came],
+            gx_send.at[0, chips + step], gx_recv.at[0, chips + step], "gx", sibling,
+        )
+        copy.start()
+        paired.append(copy)
     for copy in bc_sums:
         copy.wait()
     bc_sum = bc_rcv[0]
@@ -132,7 +169,8 @@
         )
         copy.start()
         bc_gathers.append(copy)
-    for copy in gathers:
+    flatten(1)
+    for copy in paired:
         copy.wait()
     dt_rcv[0] = lax.dot_general(
         wdt_ref[...], full[...], (((1,), (1,)), ((), ())), preferred_element_type=jnp.float32
@@ -145,29 +183,32 @@
         )
         copy.start()
         dt_sums.append(copy)
-    loads[1].wait()
-    loads[2].wait()
-
-    def tile(index, carry):
-        cols = pl.ds(pl.multiple_of(index * TILE, TILE), TILE)
-        part[:, cols] = jnp.dot(full[...], w[:, cols], preferred_element_type=jnp.float32)
-        return carry
-
-    lax.fori_loop(0, 2 * inner // TILE, tile, 0)
-    for owner in range(n_gy):
-        pieces = [
-            part[:, head * width + owner * local : head * width + (owner + 1) * local]
-            for head in range(2 * heads)
-        ]
-        snd[owner] = jnp.concatenate(pieces, axis=1).astype(jnp.bfloat16)
+
+    groups, span = snd.shape[1], part.shape[1]
     sums = []
-    for step in range(1, n_gy):
-        peer = lax.rem(gy + step, n_gy)
-        copy = remote(
-            snd.at[peer], rcv.at[step], gy_send.at[2, step], gy_recv.at[2, step], "gy", peer
-        )
-        copy.start()
-        sums.append(copy)
+    for group in range(groups):
+
+        def tile(index, carry):
+            into = pl.ds(pl.multiple_of(index * TILE, TILE), TILE)
+            cols = pl.ds(pl.multiple_of(group * span + index * TILE, TILE), TILE)
+            part[:, into] = jnp.dot(full[...], w[:, cols], preferred_element_type=jnp.float32)
+            return carry
+
+        lax.fori_loop(0, span // TILE, tile, 0)
+        for owner in range(n_gy):
+            pieces = [
+                part[:, head * width + owner * local : head * width + (owner + 1) * local]
+                for head in range(span // width)
+            ]
+            snd[owner, group] = jnp.concatenate(pieces, axis=1).astype(jnp.bfloat16)
+        for step in range(1, n_gy):
+            peer = lax.rem(gy + step, n_gy)
+            copy = remote(
+                snd.at[peer, group], rcv.at[step, group],
+                sum_send.at[group, step], sum_recv.at[group, step], "gy", peer,
+            )
+            copy.start()
+            sums.append(copy)
     for copy in bc_gathers:
         copy.wait()
     bc_ref[...] = bc_full[...]
@@ -177,19 +218,20 @@
     for step in range(1, n_gy):
         dt_sum = dt_sum + dt_rcv[step]
     dt_ref[...] = dt_sum
-    for copy in sums:
-        copy.wait()
-    total = snd[gy].astype(jnp.float32)
-    for step in range(1, n_gy):
-        total = total + rcv[step].astype(jnp.float32)
-    chan_ref[...] = total
+    lanes = snd.shape[3]
+    for group in range(groups):
+        total = snd[gy, group].astype(jnp.float32)
+        for step in range(1, n_gy):
+            sums[group * (n_gy - 1) + step - 1].wait()
+            total = total + rcv[step, group].astype(jnp.float32)
+        chan_ref[:, group * lanes : (group + 1) * lanes] = total
 
 
 def out_kernel(
     n_gx, n_gy, heads, width,
     gated_ref, gain_ref, w_ref, out_ref,
-    whole, normed, w, prod, rcv,
-    load_sem, gy_sem, gx_sem,
+    whole, normed, w, prod, paired, mixed, rcv,
+    load_sem, gy_sem, pair_sem, gx_sem,
 ):
     gx, gy = lax.axis_index("gx"), lax.axis_index("gy")
     rows, out_cols = out_ref.shape
@@ -219,28 +261,57 @@
         ).astype(jnp.bfloat16)
     load.wait()
 
-    def tile(index, carry):
-        cols = pl.ds(pl.multiple_of(index * TILE, TILE), TILE)
-        prod[:, cols] = jnp.dot(
-            normed[...], w[:, cols], preferred_element_type=jnp.float32
-        ).astype(jnp.bfloat16)
-        return carry
-
-    lax.fori_loop(0, out_cols // TILE, tile, 0)
+    core, chip, chips = gx % 2, gx // 2, n_gx // 2
+    sibling = gx + 1 - 2 * core
+    span = out_cols // CHUNKS
+
+    def block(index):
+        return pl.ds(pl.multiple_of(index * rows, rows), rows)
+
+    to_sibling = []
+    for chunk in range(CHUNKS):
+
+        def tile(index, carry):
+            cols = pl.ds(pl.multiple_of(chunk * span + index * TILE, TILE), TILE)
+            prod[:, cols] = jnp.dot(
+                normed[...], w[:, cols], preferred_element_type=jnp.float32
+            ).astype(jnp.bfloat16)
+            return carry
+
+        lax.fori_loop(0, span // TILE, tile, 0)
+        cols = pl.ds(chunk * span, span)
+        for step in range(chips):
+            other = (chip + step) % chips
+            copy = remote(
+                prod.at[block(2 * other + 1 - core), cols], paired.at[step, :, cols],
+                pair_sem.at[chunk, 0, step], pair_sem.at[chunk, 1, step], "gx", sibling,
+            )
+            copy.start()
+            to_sibling.append(copy)
     copies = []
-    for step in range(1, n_gx):
-        peer = lax.rem(gx + step, n_gx)
-        theirs = pl.ds(pl.multiple_of(peer * rows, rows), rows)
-        copy = remote(
-            prod.at[theirs], rcv.at[step], gx_sem.at[0, step], gx_sem.at[1, step], "gx", peer
-        )
-        copy.start()
-        copies.append(copy)
-    total = prod[pl.ds(pl.multiple_of(gx * rows, rows), rows)].astype(jnp.float32)
-    for step in range(1, n_gx):
-        copies[step - 1].wait()
-        total = total + rcv[step].astype(jnp.float32)
-    out_ref[...] = total.astype(jnp.bfloat16)
+    for chunk in range(CHUNKS):
+        cols = pl.ds(chunk * span, span)
+        for step in range(chips):
+            to_sibling[chunk * chips + step].wait()
+        for step in range(1, chips):
+            peer = ((chip + step) % chips) * 2 + core
+            mixed[step, :, cols] = (
+                prod[block(peer), cols].astype(jnp.float32)
+                + paired[step, :, cols].astype(jnp.float32)
+            ).astype(jnp.bfloat16)
+            copy = remote(
+                mixed.at[step, :, cols], rcv.at[step, :, cols],
+                gx_sem.at[chunk, 0, step], gx_sem.at[chunk, 1, step], "gx", peer,
+            )
+            copy.start()
+            copies.append(copy)
+    for chunk in range(CHUNKS):
+        cols = pl.ds(chunk * span, span)
+        total = prod[block(gx), cols].astype(jnp.float32) + paired[0, :, cols].astype(jnp.float32)
+        for step in range(1, chips):
+            copies[chunk * (chips - 1) + step - 1].wait()
+            total = total + rcv[step, :, cols].astype(jnp.float32)
+        out_ref[:, cols] = total.astype(jnp.bfloat16)
 
 
 def per_device(
@@ -268,6 +339,8 @@
     total = rows * n_gx
     local = head_width // n_gy
     seg = heads_here * local
+    lanes = min(LANES, 2 * seg)
+    groups = 2 * seg // lanes
     channels, bc_pre, dt_pre = pl.pallas_call(
         functools.partial(project_kernel, n_gx, n_gy, heads_here, head_width),
         out_shape=(
@@ -279,27 +352,31 @@
         out_specs=(VM, VM, VM),
         scratch_shapes=[
             pltpu.VMEM((total, d_rows), jnp.bfloat16),
+            pltpu.VMEM((2, d_rows, heads_here, head_width), jnp.bfloat16),
             pltpu.VMEM((d_rows, 2 * inner_here), jnp.bfloat16),
             pltpu.VMEM((d_rows, states_two), jnp.bfloat16),
-            pltpu.VMEM((total, 2 * inner_here), jnp.float32),
-            pltpu.VMEM((n_gy, total, 2 * seg), jnp.bfloat16),
-            pltpu.VMEM((n_gy, total, 2 * seg), jnp.bfloat16),
+            pltpu.VMEM((DEPTH * heads_here, head_width), jnp.float32),
+            pltpu.VMEM((total, 2 * inner_here // groups), jnp.float32),
+            pltpu.VMEM((n_gy, groups, total, lanes), jnp.bfloat16),
+            pltpu.VMEM((n_gy, groups, total, lanes), jnp.bfloat16),
             pltpu.VMEM((n_gy, rows, states_two), jnp.float32),
             pltpu.VMEM((total, states_two), jnp.float32),
             pltpu.VMEM((n_gy, heads_here, total), jnp.float32),
             pltpu.SemaphoreType.DMA((3,)),
             pltpu.SemaphoreType.DMA((2, n_gx)),
             pltpu.SemaphoreType.DMA((2, n_gx)),
-            pltpu.SemaphoreType.DMA((3, n_gy)),
-            pltpu.SemaphoreType.DMA((3, n_gy)),
+            pltpu.SemaphoreType.DMA((2, n_gy)),
+            pltpu.SemaphoreType.DMA((2, n_gy)),
+            pltpu.SemaphoreType.DMA((groups, n_gy)),
+            pltpu.SemaphoreType.DMA((groups, n_gy)),
         ],
         compiler_params=pltpu.CompilerParams(
             collective_id=0, has_side_effects=True, vmem_limit_bytes=48 * 1024 * 1024
         ),
     )(
         tokens,
-        w_gate.reshape(d_rows, inner_here),
-        w_x.reshape(d_rows, inner_here),
+        w_gate,
+        w_x,
         w_bc,
         w_dt.T,
     )
@@ -329,10 +406,13 @@
             pltpu.VMEM((total, inner_here), jnp.bfloat16),
             pltpu.VMEM((inner_here, out_cols), jnp.bfloat16),
             pltpu.VMEM((total, out_cols), jnp.bfloat16),
-            pltpu.VMEM((n_gx, rows, out_cols), jnp.bfloat16),
+            pltpu.VMEM((n_gx // 2, rows, out_cols), jnp.bfloat16),
+            pltpu.VMEM((n_gx // 2, rows, out_cols), jnp.bfloat16),
+            pltpu.VMEM((n_gx // 2, rows, out_cols), jnp.bfloat16),
             pltpu.SemaphoreType.DMA((1,)),
             pltpu.SemaphoreType.DMA((2, n_gy)),
-            pltpu.SemaphoreType.DMA((2, n_gx)),
+            pltpu.SemaphoreType.DMA((CHUNKS, 2, n_gx // 2)),
+            pltpu.SemaphoreType.DMA((CHUNKS, 2, n_gx // 2)),
         ],
         compiler_params=pltpu.CompilerParams(
             collective_id=1, has_side_effects=True, vmem_limit_bytes=48 * 1024 * 1024

time: 98.3 us -> 83 us (0.84)
  the two profiles are of different devices: /device:TPU:9 before, /device:TPU:0 now
where the time goes in v2:
time: 83 us; the launch traced here: 82.6 us
  Pallas kernels  67.1 us (81%)
  local copies, waits for them, and re-layouts  9.12 us (11%)
  matrix products  4.1 us (5%)
  other arithmetic  1.44 us (2%)
  between operations  0.88 us (1%)
    pallas_call x1, Pallas kernels, per_device(): pl.pallas_call(functools.partial(project_kernel, n_gx, n_gy, heads_here,...  41.5 us
    pallas_call x1, Pallas kernels, per_device(): pl.pallas_call(functools.partial(out_kernel, n_gx, n_gy, heads_here, head...  25.6 us
    unnamed x29, local copies, waits for them, and re-layouts  7.94 us
    dot_general x1, matrix products, advance(): inner = jnp.einsum('hts,shp->thp', weights, scaled, precision=high)  2.3 us

profile of v2, /device:TPU:0, one launch (start us, length us, event | category | flops | bytes accessed | tf_op | source)
XLA Modules:
  0.0 82.6 jit_solution(10996653667628374657)
XLA Ops:
  0.6 2.2 %copy-done = bf16[2048,8,128]{2,1,0:T(8,128)(2,1)S(1)} copy-done((bf16[2048,8,128]{2,1,0:T(8,128)(2,1)S(1)}, bf16[2048,8,128]{2,1,0:T(8,128)(2,1)}, u32[]{:S(2)}) %copy-start) | copy-done | bytes 4194328
  2.8 1.2 %copy-done.2 = bf16[2048,256]{1,0:T(8,128)(2,1)S(1)} copy-done((bf16[2048,256]{1,0:T(8,128)(2,1)S(1)}, bf16[2048,256]{1,0:T(8,128)(2,1)}, u32[]{:S(2)}) %copy-start.2) | copy-done | bytes 1048600
  4.1 0.9 %copy-done.3 = bf16[32,2048]{1,0:T(8,128)(2,1)S(1)} copy-done((bf16[32,2048]{1,0:T(8,128)(2,1)S(1)}, bf16[32,2048]{1,0:T(8,128)(2,1)}, u32[]{:S(2)}) %copy-start.3) | copy-done | bytes 131096
  5.0 0.8 copy-done.4
  5.7 41.5 %shard_map.158 = (f32[256,512]{1,0:T(8,128)S(1)}, f32[256,256]{1,0:T(8,128)S(1)}, f32[8,256]{1,0:T(8,128)S(1)}) custom-call(bf16[32,2048]{1,0:T(8,128)(2,1)S(1)} %copy-done.3, bf16[2048,8,128]{2,1,0:T(8,128)(2,1)S(1)} %copy-done, bf16[2048,8,128]{2,1,0:T(8,128)(2,1)} %wx_ref.1, bf16[2048,256]{1,0:T(8,128)(2,1)S(1)} %copy-done.2, bf16[8,2048]{1,0:T(8,128)(2,1)S(1)} %bitcast.42), custom_call_target="tpu_custom_call" | custom-call | tf_op jit(solution)/shard_map/pallas_call | solution.py:344
  47.3 0.2 divide_multiply_fusion
  47.5 0.4 fusion.39
  47.9 0.1 fusion.45
  48.0 0.6 reduce-window.6
  48.6 0.2 slice_reduce_fusion
  48.8 0.1 add_bitcast_fusion.1
  48.9 0.1 reshape.95
  49.0 0.1 mul.172
  49.1 0.1 mul.169
  49.2 0.1 mul.166
  49.3 0.1 mul.163
  49.3 0.2 divide_multiply_fusion.1
  49.5 0.1 copy.25
  49.6 0.1 fusion.51
  49.7 0.2 slice_reduce_fusion.1
  49.9 0.1 compare_select_fusion.1
  50.0 0.0 copy-start.5
  50.0 2.3 %fusion.6 = f32[256,8,32]{0,2,1:T(8,128)S(1)} fusion(f32[256,256]{1,0:T(8,128)S(1)} %fusion.39, f32[8,256]{1,0:T(8,128)S(1)} %add_bitcast_fusion.1, pred[256,256]{1,0:T(8,128)(4,1)S(1)} %iota_compare_fusion, f32[256,8,32]{0,2,1:T(8,128)S(1)} %bitcast.44, f32[256,8]{0,1:T(8,128)S(1)} %get-tuple-element.45), kind=kOutput, calls=%fused_computation.7 | convolution fusion | flops 202964992 | bytes 868352 | tf_op jit(solution)/shard_map/while/body/eval_jaxpr/hts,shp->thp/dot_general | solution.py:37
  52.3 0.4 fusion.5
  52.7 0.1 copy.26
  52.9 0.1 mul.197
  52.9 0.1 mul.198
  53.0 0.1 multiply_convert_fusion.gated_ref
  53.2 2.2 %copy-done.1 = bf16[8,128,2048]{2,1,0:T(8,128)(2,1)S(1)} copy-done((bf16[8,128,2048]{2,1,0:T(8,128)(2,1)S(1)}, bf16[8,128,2048]{2,1,0:T(8,128)(2,1)}, u32[]{:S(2)}) %copy-start.1) | copy-done | bytes 4194328
  55.3 25.6 %shard_map.159 = bf16[32,2048]{1,0:T(8,128)(2,1)S(1)} custom-call(bf16[256,256]{1,0:T(8,128)(2,1)S(1)} %multiply_convert_fusion.gated_ref, f32[8,128]{1,0:T(8,128)S(1)} %copy-done.5, bf16[1024,2048]{1,0:T(8,128)(2,1)S(1)} %bitcast.41), custom_call_target="tpu_custom_call" | custom-call | tf_op jit(solution)/shard_map/pallas_call | solution.py:399
  81.0 1.0 %convolution_add_fusion = f32[8,32,128]{2,1,0:T(8,128)} fusion(f32[256,8,32]{0,2,1:T(8,128)S(1)} %bitcast.45, f32[256,8]{0,1:T(8,128)S(1)} %get-tuple-element.46, f32[8,32,128]{2,1,0:T(8,128)S(1)} %copy-done.6, f32[256,8]{0,1:T(8,128)S(1)} %get-tuple-element.45, f32[256,256]{1,0:T(8,128)S(1)} %divide_multiply_fusion, f32[8]{0:T(128)S(1)} %exp.44), kind=kOutput, calls=%fused_computation.8 | convolution fusion | flops 100859904 | bytes 672256 | tf_op jit(solution)/shard_map/while/body/eval_jaxpr/sh,shp,sn->hpn/dot_general | solution.py:40
  82.0 0.7 copy.28
  (29 shorter events, 0.1 us)
Async XLA Ops:
  0.6 2.2 %copy-start = (bf16[2048,8,128]{2,1,0:T(8,128)(2,1)S(1)}, bf16[2048,8,128]{2,1,0:T(8,128)(2,1)}, u32[]{:S(2)}) copy-start(bf16[2048,8,128]{2,1,0:T(8,128)(2,1)} %wg_ref.1) | copy-start | bytes 12582916
  2.8 1.2 %copy-start.2 = (bf16[2048,256]{1,0:T(8,128)(2,1)S(1)}, bf16[2048,256]{1,0:T(8,128)(2,1)}, u32[]{:S(2)}) copy-start(bf16[2048,256]{1,0:T(8,128)(2,1)} %wbc_ref.1) | copy-start | bytes 3145732
  4.0 0.9 %copy-start.3 = (bf16[32,2048]{1,0:T(8,128)(2,1)S(1)}, bf16[32,2048]{1,0:T(8,128)(2,1)}, u32[]{:S(2)}) copy-start(bf16[32,2048]{1,0:T(8,128)(2,1)} %tok_ref.1) | copy-start | bytes 393220
  5.0 0.8 copy-start.4
  5.7 41.6 %copy-start.10 = (f32[4,256]{1,0:T(4,128)S(1)}, f32[4,256]{1,0:T(4,128)}, u32[]{:S(2)}) copy-start(f32[4,256]{1,0:T(4,128)} %param.21) | copy-start | bytes 12292
  5.7 41.6 %copy-start.9 = (f32[3,256]{1,0:T(4,128)S(1)}, f32[3,256]{1,0:T(4,128)}, u32[]{:S(2)}) copy-start(f32[3,256]{1,0:T(4,128)} %param.23) | copy-start | bytes 9220
  5.7 42.2 %copy-start.11 = (f32[8]{0:T(128)S(1)}, f32[8]{0:T(128)}, u32[]{:S(2)}) copy-start(f32[8]{0:T(128)} %param.24) | copy-start | bytes 100
  5.7 42.2 %copy-start.12 = (f32[8]{0:T(128)S(1)}, f32[8]{0:T(128)}, u32[]{:S(2)}) copy-start(f32[8]{0:T(128)} %param.25) | copy-start | bytes 100
  5.7 43.2 %copy-start.8 = (f32[3,8,32]{2,1,0:T(8,128)S(1)}, f32[3,8,32]{2,1,0:T(8,128)}, u32[]{:S(2)}) copy-start(f32[3,8,32]{2,1,0:T(8,128)} %param.22) | copy-start | bytes 9220
  5.7 43.3 %copy-start.7 = (f32[4,8,32]{2,1,0:T(8,128)S(1)}, f32[4,8,32]{2,1,0:T(8,128)}, u32[]{:S(2)}) copy-start(f32[4,8,32]{2,1,0:T(8,128)} %param.20) | copy-start | bytes 12292
  48.9 3.4 %copy-start.6 = (f32[8,32,128]{2,1,0:T(8,128)S(1)}, f32[8,32,128]{2,1,0:T(8,128)}, u32[]{:S(2)}) copy-start(f32[8,32,128]{2,1,0:T(8,128)} %param.27) | copy-start | bytes 393220
  49.7 3.1 %copy-start.13 = (f32[8]{0:T(128)S(1)}, f32[8]{0:T(128)}, u32[]{:S(2)}) copy-start(f32[8]{0:T(128)} %param.26) | copy-start | bytes 100
  50.0 3.1 %copy-start.5 = (f32[8,128]{1,0:T(8,128)S(1)}, f32[8,128]{1,0:T(8,128)}, u32[]{:S(2)}) copy-start(f32[8,128]{1,0:T(8,128)} %gain_ref.1) | copy-start | bytes 12292
  53.2 2.2 %copy-start.1 = (bf16[8,128,2048]{2,1,0:T(8,128)(2,1)S(1)}, bf16[8,128,2048]{2,1,0:T(8,128)(2,1)}, u32[]{:S(2)}) copy-start(bf16[8,128,2048]{2,1,0:T(8,128)(2,1)} %param.29) | copy-start | bytes 12582916

commit v3 on v2

--- a/solution.py
+++ b/solution.py
@@ -53,7 +53,7 @@
 
 
 VM = pl.BlockSpec(memory_space=pltpu.VMEM)
-HBM = pl.BlockSpec(memory_space=pl.ANY)
+HBM = pl.BlockSpec(memory_space=pltpu.HBM)
 MESH = pl.DeviceIdType.MESH
 TILE = 256
 DEPTH = 128
@@ -371,7 +371,7 @@
             pltpu.SemaphoreType.DMA((groups, n_gy)),
         ],
         compiler_params=pltpu.CompilerParams(
-            collective_id=0, has_side_effects=True, vmem_limit_bytes=48 * 1024 * 1024
+            collective_id=0, has_side_effects=True, vmem_limit_bytes=56 * 1024 * 1024
         ),
     )(
         tokens,
@@ -415,7 +415,7 @@
             pltpu.SemaphoreType.DMA((CHUNKS, 2, n_gx // 2)),
         ],
         compiler_params=pltpu.CompilerParams(
-            collective_id=1, has_side_effects=True, vmem_limit_bytes=48 * 1024 * 1024
+            collective_id=1, has_side_effects=True, vmem_limit_bytes=56 * 1024 * 1024
         ),
     )(gated, norm_gain, w_out.reshape(inner_here, out_cols))
     return (summed, state_out)

time: 83 us -> 82.9 us (level)
  local copies, waits for them, and re-layouts: 9.12 us -> 3.74 us
  Pallas kernels: 67.1 us -> 69.8 us
  other arithmetic: 1.44 us -> 4.14 us
    unnamed x29 -> x21, local copies, waits for them, and re-layouts: 7.94 us -> 1.61 us
    pallas_call x1, Pallas kernels: 41.5 us -> 42.9 us  [per_device(): pl.pallas_call(functools.partial(project_kernel, n_gx, n_gy, heads_here,...]
    mul x2, other arithmetic: 0.35 us -> 1.73 us  [conv_silu(): return jax.nn.silu(acc)]
    pallas_call x1, Pallas kernels: 25.6 us -> 26.8 us  [per_device(): pl.pallas_call(functools.partial(out_kernel, n_gx, n_gy, heads_here, head...]
    slice x1, local copies, waits for them, and re-layouts: 0.02 us -> 0.97 us  [per_device(): channels[:, seg:]]
where the time goes in v3:
time: 82.9 us; the launch traced here: 82.6 us
  Pallas kernels  69.8 us (84%)
  other arithmetic  4.14 us (5%)
  matrix products  4.1 us (5%)
  local copies, waits for them, and re-layouts  3.74 us (5%)
  between operations  0.87 us (1%)
    pallas_call x1, Pallas kernels, per_device(): pl.pallas_call(functools.partial(project_kernel, n_gx, n_gy, heads_here,...  42.9 us
    pallas_call x1, Pallas kernels, per_device(): pl.pallas_call(functools.partial(out_kernel, n_gx, n_gy, heads_here, head...  26.8 us
    dot_general x1, matrix products, advance(): inner = jnp.einsum('hts,shp->thp', weights, scaled, precision=high)  2.3 us
    mul x2, other arithmetic, conv_silu(): return jax.nn.silu(acc)  1.73 us

profile of v3, /device:TPU:0, one launch (start us, length us, event | category | flops | bytes accessed | tf_op | source)
XLA Modules:
  0.0 82.6 jit_solution(14726338084174687740)
XLA Ops:
  0.6 0.0 copy-start.6
  0.6 0.0 copy-start.5
  0.7 0.0 copy-start.7
  0.7 0.0 copy-start.8
  0.7 42.9 %shard_map.158 = (f32[256,512]{1,0:T(8,128)}, f32[256,256]{1,0:T(8,128)}, f32[8,256]{1,0:T(8,128)}) custom-call(bf16[32,2048]{1,0:T(8,128)(2,1)} %tok_ref.1, bf16[2048,8,128]{2,1,0:T(8,128)(2,1)} %wg_ref.1, bf16[2048,8,128]{2,1,0:T(8,128)(2,1)} %wx_ref.1, bf16[2048,256]{1,0:T(8,128)(2,1)} %wbc_ref.1, bf16[8,2048]{1,0:T(8,128)(2,1)} %bitcast.45), custom_call_target="tpu_custom_call" | custom-call | tf_op jit(solution)/shard_map/pallas_call | solution.py:344
  43.7 1.6 %divide_multiply_fusion = f32[256,256]{1,0:T(8,128)S(1)} fusion(f32[256,256]{1,0:T(8,128)} %get-tuple-element.25, f32[3,256]{1,0:T(4,128)S(1)} %copy-done.5, f32[256]{0:T(256)S(1)} %bitcast.48, f32[256]{0:T(256)S(1)} %bitcast.49, f32[256]{0:T(256)S(1)} %bitcast.47, f32[256]{0:T(256)S(1)} %bitcast.46), kind=kLoop, calls=%fused_computation.38 | loop fusion | flops 917504 | bytes 531456 | tf_op jit(solution)/shard_map/jit(silu)/mul | solution.py:19
  45.2 0.4 fusion.39
  45.6 0.8 fusion.45
  46.4 0.6 reduce-window.6
  47.0 0.2 slice_reduce_fusion
  47.2 0.1 add_bitcast_fusion.1
  47.3 1.0 %slice.70 = f32[256,256]{1,0:T(8,128)S(1)} slice(f32[256,512]{1,0:T(8,128)} %get-tuple-element.23), slice={[0:256], [256:512]} | slice | bytes 524288 | tf_op jit(solution)/shard_map/slice | solution.py:386
  48.3 0.0 copy-start
  48.3 0.1 reshape.95
  48.4 0.1 mul.172
  48.5 0.1 mul.169
  48.6 0.1 mul.166
  48.6 0.1 mul.163
  48.7 0.2 divide_multiply_fusion.1
  48.9 0.1 copy.25
  49.0 0.1 fusion.51
  49.1 0.2 slice_reduce_fusion.1
  49.3 0.1 compare_select_fusion.1
  49.4 2.3 %fusion.6 = f32[256,8,32]{0,2,1:T(8,128)S(1)} fusion(f32[256,256]{1,0:T(8,128)S(1)} %fusion.39, f32[8,256]{1,0:T(8,128)S(1)} %add_bitcast_fusion.1, pred[256,256]{1,0:T(8,128)(4,1)S(1)} %iota_compare_fusion, f32[256,8,32]{0,2,1:T(8,128)S(1)} %bitcast.43, f32[256,8]{0,1:T(8,128)S(1)} %get-tuple-element.45), kind=kOutput, calls=%fused_computation.7 | convolution fusion | flops 202964992 | bytes 868352 | tf_op jit(solution)/shard_map/while/body/eval_jaxpr/hts,shp->thp/dot_general | solution.py:37
  51.7 0.4 fusion.5
  52.1 0.1 copy.26
  52.2 0.1 mul.197
  52.3 0.1 mul.198
  52.4 0.7 multiply_convert_fusion.gated_ref
  53.1 26.8 %shard_map.159 = bf16[32,2048]{1,0:T(8,128)(2,1)} custom-call(bf16[256,256]{1,0:T(8,128)(2,1)} %multiply_convert_fusion.gated_ref, f32[8,128]{1,0:T(8,128)} %gain_ref.1, bf16[1024,2048]{1,0:T(8,128)(2,1)} %bitcast.41), custom_call_target="tpu_custom_call" | custom-call | tf_op jit(solution)/shard_map/pallas_call | solution.py:399
  80.0 1.0 %convolution_add_fusion = f32[8,32,128]{2,1,0:T(8,128)} fusion(f32[256,8,32]{0,2,1:T(8,128)S(1)} %bitcast.44, f32[256,8]{0,1:T(8,128)S(1)} %get-tuple-element.46, f32[8,32,128]{2,1,0:T(8,128)S(1)} %copy-done, f32[256,8]{0,1:T(8,128)S(1)} %get-tuple-element.45, f32[256,256]{1,0:T(8,128)S(1)} %divide_multiply_fusion, f32[8]{0:T(128)S(1)} %exp.44), kind=kOutput, calls=%fused_computation.8 | convolution fusion | flops 100859904 | bytes 672256 | tf_op jit(solution)/shard_map/while/body/eval_jaxpr/sh,shp,sn->hpn/dot_general | solution.py:40
  81.0 1.6 %copy.28 = bf16[32,2048]{1,0:T(8,128)(2,1)} copy(bf16[32,2048]{1,0:T(8,128)(2,1)} %shard_map.159) | data formatting | bytes 262144
  (21 shorter events, 0.1 us)
Async XLA Ops:
  0.6 43.0 %copy-start.6 = (f32[4,256]{1,0:T(4,128)S(1)}, f32[4,256]{1,0:T(4,128)}, u32[]{:S(2)}) copy-start(f32[4,256]{1,0:T(4,128)} %param.21) | copy-start | bytes 12292
  0.6 43.0 %copy-start.5 = (f32[3,256]{1,0:T(4,128)S(1)}, f32[3,256]{1,0:T(4,128)}, u32[]{:S(2)}) copy-start(f32[3,256]{1,0:T(4,128)} %param.23) | copy-start | bytes 9220
  0.7 45.0 %copy-start.7 = (f32[8]{0:T(128)S(1)}, f32[8]{0:T(128)}, u32[]{:S(2)}) copy-start(f32[8]{0:T(128)} %param.24) | copy-start | bytes 100
  0.7 45.0 %copy-start.8 = (f32[8]{0:T(128)S(1)}, f32[8]{0:T(128)}, u32[]{:S(2)}) copy-start(f32[8]{0:T(128)} %param.25) | copy-start | bytes 100
  0.7 47.6 %copy-start.4 = (f32[3,8,32]{2,1,0:T(8,128)S(1)}, f32[3,8,32]{2,1,0:T(8,128)}, u32[]{:S(2)}) copy-start(f32[3,8,32]{2,1,0:T(8,128)} %param.22) | copy-start | bytes 9220
  0.7 47.7 %copy-start.3 = (f32[4,8,32]{2,1,0:T(8,128)S(1)}, f32[4,8,32]{2,1,0:T(8,128)}, u32[]{:S(2)}) copy-start(f32[4,8,32]{2,1,0:T(8,128)} %param.20) | copy-start | bytes 12292
  43.6 5.7 %copy-start.2 = (f32[8,256]{1,0:T(8,128)S(1)}, f32[8,256]{1,0:T(8,128)}, u32[]{:S(2)}) copy-start(f32[8,256]{1,0:T(8,128)} %get-tuple-element.24) | copy-start | bytes 24580
  48.3 3.4 %copy-start = (f32[8,32,128]{2,1,0:T(8,128)S(1)}, f32[8,32,128]{2,1,0:T(8,128)}, u32[]{:S(2)}) copy-start(f32[8,32,128]{2,1,0:T(8,128)} %param.27) | copy-start | bytes 393220
  49.1 3.1 %copy-start.9 = (f32[8]{0:T(128)S(1)}, f32[8]{0:T(128)}, u32[]{:S(2)}) copy-start(f32[8]{0:T(128)} %param.26) | copy-start | bytes 100
  49.1 3.3 %copy-start.1 = (f32[256,512]{1,0:T(8,128)S(1)}, f32[256,512]{1,0:T(8,128)}, u32[]{:S(2)}) copy-start(f32[256,512]{1,0:T(8,128)} %get-tuple-element.23) | copy-start | bytes 1572868

commit v4 on v3

--- a/solution.py
+++ b/solution.py
@@ -85,7 +85,7 @@
 def project_kernel(
     n_gx, n_gy, heads, width,
     tok_ref, wg_ref, wx_ref, wbc_ref, wdt_ref,
-    chan_ref, bc_ref, dt_ref,
+    gate_ref, x_ref, bc_ref, dt_ref,
     full, raw, w, wbc, spread, part, snd, rcv, bc_rcv, bc_full, dt_rcv,
     load_sem, gx_send, gx_recv, gy_send, gy_recv, sum_send, sum_recv,
 ):
@@ -169,7 +169,6 @@
         )
         copy.start()
         bc_gathers.append(copy)
-    flatten(1)
     for copy in paired:
         copy.wait()
     dt_rcv[0] = lax.dot_general(
@@ -186,7 +185,11 @@
 
     groups, span = snd.shape[1], part.shape[1]
     sums = []
+    if groups == 1:
+        flatten(1)
     for group in range(groups):
+        if groups > 1 and group == groups // 2:
+            flatten(1)
 
         def tile(index, carry):
             into = pl.ds(pl.multiple_of(index * TILE, TILE), TILE)
@@ -218,13 +221,17 @@
     for step in range(1, n_gy):
         dt_sum = dt_sum + dt_rcv[step]
     dt_ref[...] = dt_sum
-    lanes = snd.shape[3]
+    totals = []
     for group in range(groups):
         total = snd[gy, group].astype(jnp.float32)
         for step in range(1, n_gy):
             sums[group * (n_gy - 1) + step - 1].wait()
             total = total + rcv[step, group].astype(jnp.float32)
-        chan_ref[:, group * lanes : (group + 1) * lanes] = total
+        totals.append(total)
+    both = jnp.concatenate(totals, axis=1) if groups > 1 else totals[0]
+    seg = heads * local
+    gate_ref[...] = both[:, :seg]
+    x_ref[...] = both[:, seg:]
 
 
 def out_kernel(
@@ -239,26 +246,36 @@
     load = pltpu.make_async_copy(w_ref, w, load_sem.at[0])
     load.start()
     greet(n_gx, n_gy)
+    parts = gy_sem.shape[0]
+    lanes, held = heads * local // parts, heads // parts
     copies = []
-    for step in range(1, n_gy):
-        peer = lax.rem(gy + step, n_gy)
-        copy = remote(
-            gated_ref, whole.at[gy], gy_sem.at[0, step], gy_sem.at[1, step], "gy", peer
-        )
-        copy.start()
-        copies.append(copy)
+    for piece in range(parts):
+        for step in range(1, n_gy):
+            peer = lax.rem(gy + step, n_gy)
+            cols = pl.ds(piece * lanes, lanes)
+            copy = remote(
+                gated_ref.at[:, cols], whole.at[gy, :, cols],
+                gy_sem.at[piece, 0, step], gy_sem.at[piece, 1, step], "gy", peer,
+            )
+            copy.start()
+            copies.append(copy)
     whole[gy] = gated_ref[...]
-    for copy in copies:
-        copy.wait()
-    blocks = [whole[owner].astype(jnp.float32) for owner in range(n_gy)]
-    for head in range(heads):
-        row = jnp.concatenate(
-            [block[:, head * local : (head + 1) * local] for block in blocks], axis=1
-        )
-        mean = jnp.mean(row * row, axis=1, keepdims=True)
-        normed[:, head * width : (head + 1) * width] = (
-            row * lax.rsqrt(mean + 1e-05) * gain_ref[head : head + 1, :]
-        ).astype(jnp.bfloat16)
+    for piece in range(parts):
+        for step in range(1, n_gy):
+            copies[piece * (n_gy - 1) + step - 1].wait()
+        blocks = [
+            whole[owner, :, piece * lanes : (piece + 1) * lanes].astype(jnp.float32)
+            for owner in range(n_gy)
+        ]
+        for index in range(held):
+            head = piece * held + index
+            row = jnp.concatenate(
+                [block[:, index * local : (index + 1) * local] for block in blocks], axis=1
+            )
+            mean = jnp.mean(row * row, axis=1, keepdims=True)
+            normed[:, head * width : (head + 1) * width] = (
+                row * lax.rsqrt(mean + 1e-05) * gain_ref[head : head + 1, :]
+            ).astype(jnp.bfloat16)
     load.wait()
 
     core, chip, chips = gx % 2, gx // 2, n_gx // 2
@@ -341,15 +358,16 @@
     seg = heads_here * local
     lanes = min(LANES, 2 * seg)
     groups = 2 * seg // lanes
-    channels, bc_pre, dt_pre = pl.pallas_call(
+    gate_pre, x_pre, bc_pre, dt_pre = pl.pallas_call(
         functools.partial(project_kernel, n_gx, n_gy, heads_here, head_width),
         out_shape=(
-            jax.ShapeDtypeStruct((total, 2 * seg), jnp.float32),
+            jax.ShapeDtypeStruct((total, seg), jnp.float32),
+            jax.ShapeDtypeStruct((total, seg), jnp.float32),
             jax.ShapeDtypeStruct((total, states_two), jnp.float32),
             jax.ShapeDtypeStruct((heads_here, total), jnp.float32),
         ),
         in_specs=[VM, HBM, HBM, HBM, VM],
-        out_specs=(VM, VM, VM),
+        out_specs=(VM, VM, VM, VM),
         scratch_shapes=[
             pltpu.VMEM((total, d_rows), jnp.bfloat16),
             pltpu.VMEM((2, d_rows, heads_here, head_width), jnp.bfloat16),
@@ -380,10 +398,9 @@
         w_bc,
         w_dt.T,
     )
-    gate_pre = channels[:, :seg]
     taps = conv_x_w.shape[0]
     flat_values = conv_silu(
-        channels[:, seg:], conv_x_state.reshape(taps - 1, seg), conv_x_w.reshape(taps, seg)
+        x_pre, conv_x_state.reshape(taps - 1, seg), conv_x_w.reshape(taps, seg)
     )
     values = flat_values.reshape(total, heads_here, local)
     bc_conv = conv_silu(bc_pre, conv_bc_state, conv_bc_w)
@@ -410,7 +427,7 @@
             pltpu.VMEM((n_gx // 2, rows, out_cols), jnp.bfloat16),
             pltpu.VMEM((n_gx // 2, rows, out_cols), jnp.bfloat16),
             pltpu.SemaphoreType.DMA((1,)),
-            pltpu.SemaphoreType.DMA((2, n_gy)),
+            pltpu.SemaphoreType.DMA((max(1, seg // LANES), 2, n_gy)),
             pltpu.SemaphoreType.DMA((CHUNKS, 2, n_gx // 2)),
             pltpu.SemaphoreType.DMA((CHUNKS, 2, n_gx // 2)),
         ],

time: 82.9 us -> 82.3 us (level)
  local copies, waits for them, and re-layouts: 3.74 us -> 2.77 us
    pallas_call x1, Pallas kernels: 26.8 us -> 27.9 us  [per_device(): pl.pallas_call(functools.partial(out_kernel, n_gx, n_gy, heads_here, head...]
    pallas_call x1, Pallas kernels: 42.9 us -> 41.9 us  [per_device(): pl.pallas_call(functools.partial(project_kernel, n_gx, n_gy, heads_here,...]
    slice x1 -> x0, local copies, waits for them, and re-layouts: 0.97 us -> none  [per_device(): channels[:, seg:]]
    mul x2 -> x1, other arithmetic: 1.73 us -> 2.12 us  [conv_silu(): return jax.nn.silu(acc)]
where the time goes in v4:
time: 82.3 us; the launch traced here: 82 us
  Pallas kernels  69.8 us (85%)
  other arithmetic  4.52 us (5%)
  matrix products  4.1 us (5%)
  local copies, waits for them, and re-layouts  2.77 us (3%)
  between operations  0.86 us (1%)
    pallas_call x1, Pallas kernels, per_device(): pl.pallas_call(functools.partial(project_kernel, n_gx, n_gy, heads_here,...  41.9 us
    pallas_call x1, Pallas kernels, per_device(): pl.pallas_call(functools.partial(out_kernel, n_gx, n_gy, heads_here, head...  27.9 us
    dot_general x1, matrix products, advance(): inner = jnp.einsum('hts,shp->thp', weights, scaled, precision=high)  2.29 us
    mul x1, other arithmetic, conv_silu(): return jax.nn.silu(acc)  2.12 us

profile of v4, /device:TPU:0, one launch (start us, length us, event | category | flops | bytes accessed | tf_op | source)
XLA Modules:
  0.0 82.0 jit_solution(9830828800128581766)
XLA Ops:
  0.6 0.0 copy-start.6
  0.6 0.0 copy-start.3
  0.7 0.0 copy-start.4
  0.7 0.0 copy-start.5
  0.7 0.0 copy-start.7
  0.7 0.0 copy-start.8
  0.7 41.9 %shard_map.158 = (f32[256,256]{1,0:T(8,128)}, f32[256,256]{1,0:T(8,128)}, f32[256,256]{1,0:T(8,128)}, f32[8,256]{1,0:T(8,128)}) custom-call(bf16[32,2048]{1,0:T(8,128)(2,1)} %tok_ref.1, bf16[2048,8,128]{2,1,0:T(8,128)(2,1)} %wg_ref.1, bf16[2048,8,128]{2,1,0:T(8,128)(2,1)} %wx_ref.1, bf16[2048,256]{1,0:T(8,128)(2,1)} %wbc_ref.1, bf16[8,2048]{1,0:T(8,128)(2,1)} %bitcast.45), custom_call_target="tpu_custom_call" | custom-call | tf_op jit(solution)/shard_map/pallas_call | solution.py:361
  42.6 0.1 mul.172
  42.7 0.1 reshape.95
  42.8 0.1 mul.169
  42.8 0.1 mul.166
  42.9 0.1 mul.163
  43.0 2.1 %divide_multiply_fusion = (f32[256,256]{1,0:T(8,128)S(1)}, f32[256,256]{1,0:T(8,128)S(1)}) fusion(f32[256,256]{1,0:T(8,128)} %get-tuple-element.26, f32[3,256]{1,0:T(4,128)S(1)} %copy-done.5, f32[256]{0:T(256)S(1)} %bitcast.48, f32[256]{0:T(256)S(1)} %bitcast.49, f32[256]{0:T(256)S(1)} %bitcast.47, f32[256]{0:T(256)S(1)} %bitcast.46, ...), kind=kLoop, calls=%fused_computation.38 | loop fusion | flops 1835008 | bytes 1062912 | tf_op jit(solution)/shard_map/jit(silu)/mul | solution.py:19
  45.1 0.0 copy-start
  45.1 0.4 fusion.39
  45.5 0.8 fusion.45
  46.3 0.6 reduce-window.6
  46.9 0.2 slice_reduce_fusion
  47.1 0.1 add_bitcast_fusion.1
  47.2 0.1 copy.25
  47.4 0.1 fusion.51
  47.5 0.2 slice_reduce_fusion.1
  47.6 0.1 compare_select_fusion.1
  47.7 2.3 %fusion.6 = f32[256,8,32]{0,2,1:T(8,128)S(1)} fusion(f32[256,256]{1,0:T(8,128)S(1)} %fusion.39, f32[8,256]{1,0:T(8,128)S(1)} %add_bitcast_fusion.1, pred[256,256]{1,0:T(8,128)(4,1)S(1)} %iota_compare_fusion, f32[256,8,32]{0,2,1:T(8,128)S(1)} %bitcast.43, f32[256,8]{0,1:T(8,128)S(1)} %get-tuple-element.49), kind=kOutput, calls=%fused_computation.7 | convolution fusion | flops 202964992 | bytes 868352 | tf_op jit(solution)/shard_map/while/body/eval_jaxpr/hts,shp->thp/dot_general | solution.py:37
  50.0 0.4 fusion.5
  50.4 0.1 copy.26
  50.6 0.1 mul.197
  50.6 0.1 mul.198
  50.7 0.7 multiply_convert_fusion.gated_ref
  51.5 27.9 %shard_map.159 = bf16[32,2048]{1,0:T(8,128)(2,1)} custom-call(bf16[256,256]{1,0:T(8,128)(2,1)} %multiply_convert_fusion.gated_ref, f32[8,128]{1,0:T(8,128)} %gain_ref.1, bf16[1024,2048]{1,0:T(8,128)(2,1)} %bitcast.41), custom_call_target="tpu_custom_call" | custom-call | tf_op jit(solution)/shard_map/pallas_call | solution.py:416
  79.4 1.0 %convolution_add_fusion = f32[8,32,128]{2,1,0:T(8,128)} fusion(f32[256,8,32]{0,2,1:T(8,128)S(1)} %bitcast.44, f32[256,8]{0,1:T(8,128)S(1)} %get-tuple-element.50, f32[8,32,128]{2,1,0:T(8,128)S(1)} %copy-done, f32[256,8]{0,1:T(8,128)S(1)} %get-tuple-element.49, f32[256,256]{1,0:T(8,128)S(1)} %get-tuple-element.47, f32[8]{0:T(128)S(1)} %exp.44), kind=kOutput, calls=%fused_computation.8 | convolution fusion | flops 100859904 | bytes 672256 | tf_op jit(solution)/shard_map/while/body/eval_jaxpr/sh,shp,sn->hpn/dot_general | solution.py:40
  80.5 1.6 %copy.28 = bf16[32,2048]{1,0:T(8,128)(2,1)} copy(bf16[32,2048]{1,0:T(8,128)(2,1)} %shard_map.159) | data formatting | bytes 262144
  (19 shorter events, 0.1 us)
Async XLA Ops:
  0.6 41.9 %copy-start.6 = (f32[4,256]{1,0:T(4,128)S(1)}, f32[4,256]{1,0:T(4,128)}, u32[]{:S(2)}) copy-start(f32[4,256]{1,0:T(4,128)} %param.21) | copy-start | bytes 12292
  0.6 41.9 %copy-start.3 = (f32[4,8,32]{2,1,0:T(8,128)S(1)}, f32[4,8,32]{2,1,0:T(8,128)}, u32[]{:S(2)}) copy-start(f32[4,8,32]{2,1,0:T(8,128)} %param.20) | copy-start | bytes 12292
  0.7 42.0 %copy-start.4 = (f32[3,8,32]{2,1,0:T(8,128)S(1)}, f32[3,8,32]{2,1,0:T(8,128)}, u32[]{:S(2)}) copy-start(f32[3,8,32]{2,1,0:T(8,128)} %param.22) | copy-start | bytes 9220
  0.7 42.3 %copy-start.5 = (f32[3,256]{1,0:T(4,128)S(1)}, f32[3,256]{1,0:T(4,128)}, u32[]{:S(2)}) copy-start(f32[3,256]{1,0:T(4,128)} %param.23) | copy-start | bytes 9220
  0.7 44.9 %copy-start.7 = (f32[8]{0:T(128)S(1)}, f32[8]{0:T(128)}, u32[]{:S(2)}) copy-start(f32[8]{0:T(128)} %param.24) | copy-start | bytes 100
  0.7 44.9 %copy-start.8 = (f32[8]{0:T(128)S(1)}, f32[8]{0:T(128)}, u32[]{:S(2)}) copy-start(f32[8]{0:T(128)} %param.25) | copy-start | bytes 100
  42.6 5.1 %copy-start.2 = (f32[8,256]{1,0:T(8,128)S(1)}, f32[8,256]{1,0:T(8,128)}, u32[]{:S(2)}) copy-start(f32[8,256]{1,0:T(8,128)} %get-tuple-element.25) | copy-start | bytes 24580
  45.1 4.9 %copy-start = (f32[8,32,128]{2,1,0:T(8,128)S(1)}, f32[8,32,128]{2,1,0:T(8,128)}, u32[]{:S(2)}) copy-start(f32[8,32,128]{2,1,0:T(8,128)} %param.27) | copy-start | bytes 393220
  47.4 3.1 %copy-start.9 = (f32[8]{0:T(128)S(1)}, f32[8]{0:T(128)}, u32[]{:S(2)}) copy-start(f32[8]{0:T(128)} %param.26) | copy-start | bytes 100
  47.4 3.3 %copy-start.1 = (f32[256,256]{1,0:T(8,128)S(1)}, f32[256,256]{1,0:T(8,128)}, u32[]{:S(2)}) copy-start(f32[256,256]{1,0:T(8,128)} %get-tuple-element.36) | copy-start | bytes 786436

commit v5 on v4

--- a/solution.py
+++ b/solution.py
@@ -34,10 +34,10 @@
         decay = jnp.exp(jnp.where(lower[None], gap, -jnp.inf))
         weights = decay * scores[None]
         scaled = vals * dl[:, :, None]
-        inner = jnp.einsum("hts,shp->thp", weights, scaled, precision=high)
-        carried = jnp.exp(cum)[:, :, None] * jnp.einsum("tn,hpn->thp", cm, carry, precision=high)
+        inner = jnp.einsum("hts,shp->thp", weights, scaled)
+        carried = jnp.exp(cum)[:, :, None] * jnp.einsum("tn,hpn->thp", cm, carry)
         tail = jnp.exp(cum[-1][None, :] - cum)
-        update = jnp.einsum("sh,shp,sn->hpn", tail, scaled, bm, precision=high)
+        update = jnp.einsum("sh,shp,sn->hpn", tail, scaled, bm)
         new_state = jnp.exp(cum[-1])[:, None, None] * carry + update
         return (new_state, inner + carried)
 

time: 82.3 us -> 80.2 us (0.974)
  matrix products: 4.1 us -> 2.03 us
    dot_general x3, matrix products: 3.72 us -> 1.65 us  [the longest x1 0.84 us: advance(): update = jnp.einsum('sh,shp,sn->hpn', tail, scaled, bm)]
where the time goes in v5:
time: 80.2 us; the launch traced here: 80 us
  Pallas kernels  69.8 us (87%)
  other arithmetic  4.52 us (6%)
  local copies, waits for them, and re-layouts  2.77 us (3%)
  matrix products  2.03 us (3%)
  between operations  0.87 us (1%)
    pallas_call x1, Pallas kernels, per_device(): pl.pallas_call(functools.partial(project_kernel, n_gx, n_gy, heads_here,...  41.9 us
    pallas_call x1, Pallas kernels, per_device(): pl.pallas_call(functools.partial(out_kernel, n_gx, n_gy, heads_here, head...  28 us
    mul x1, other arithmetic, conv_silu(): return jax.nn.silu(acc)  2.12 us
    unnamed x21, local copies, waits for them, and re-layouts  1.61 us

profile of v5, /device:TPU:0, one launch (start us, length us, event | category | flops | bytes accessed | tf_op | source)
XLA Modules:
  0.0 80.0 jit_solution(4593249130049102885)
XLA Ops:
  0.6 0.0 copy-start.6
  0.6 0.0 copy-start.3
  0.7 41.9 %shard_map.158 = (f32[256,256]{1,0:T(8,128)}, f32[256,256]{1,0:T(8,128)}, f32[256,256]{1,0:T(8,128)}, f32[8,256]{1,0:T(8,128)}) custom-call(bf16[32,2048]{1,0:T(8,128)(2,1)} %tok_ref.1, bf16[2048,8,128]{2,1,0:T(8,128)(2,1)} %wg_ref.1, bf16[2048,8,128]{2,1,0:T(8,128)(2,1)} %wx_ref.1, bf16[2048,256]{1,0:T(8,128)(2,1)} %wbc_ref.1, bf16[8,2048]{1,0:T(8,128)(2,1)} %bitcast.45), custom_call_target="tpu_custom_call" | custom-call | tf_op jit(solution)/shard_map/pallas_call | solution.py:361
  42.6 0.1 mul.172
  42.7 0.1 reshape.95
  42.8 0.1 mul.169
  42.8 0.1 mul.166
  42.9 0.1 mul.163
  43.0 2.1 %divide_multiply_fusion = (f32[256,256]{1,0:T(8,128)S(1)}, f32[256,256]{1,0:T(8,128)S(1)}) fusion(f32[256,256]{1,0:T(8,128)} %get-tuple-element.26, f32[3,256]{1,0:T(4,128)S(1)} %copy-done.5, f32[256]{0:T(256)S(1)} %bitcast.48, f32[256]{0:T(256)S(1)} %bitcast.49, f32[256]{0:T(256)S(1)} %bitcast.47, f32[256]{0:T(256)S(1)} %bitcast.46, ...), kind=kLoop, calls=%fused_computation.38 | loop fusion | flops 1835008 | bytes 1062912 | tf_op jit(solution)/shard_map/jit(silu)/mul | solution.py:19
  45.1 0.0 copy-start
  45.1 0.4 fusion.39
  45.5 0.8 fusion.45
  46.3 0.6 reduce-window.6
  46.9 0.2 slice_reduce_fusion
  47.1 0.1 add_bitcast_fusion.1
  47.2 0.1 copy.25
  47.4 0.1 fusion.51
  47.4 0.2 slice_reduce_fusion.1
  47.6 0.0 copy-start.9
  47.6 0.1 compare_select_fusion.1
  47.7 0.6 fusion.6
  48.4 0.0 copy-done
  48.4 0.2 fusion.5
  48.6 0.1 copy.26
  48.7 0.0 copy-done.9
  48.7 0.1 mul.197
  48.8 0.1 mul.198
  48.9 0.0 copy-done.1
  48.9 0.7 multiply_convert_fusion.gated_ref
  49.6 28.0 %shard_map.159 = bf16[32,2048]{1,0:T(8,128)(2,1)} custom-call(bf16[256,256]{1,0:T(8,128)(2,1)} %multiply_convert_fusion.gated_ref, f32[8,128]{1,0:T(8,128)} %gain_ref.1, bf16[1024,2048]{1,0:T(8,128)(2,1)} %bitcast.41), custom_call_target="tpu_custom_call" | custom-call | tf_op jit(solution)/shard_map/pallas_call | solution.py:416
  77.6 0.8 %convolution_add_fusion = f32[8,32,128]{2,1,0:T(8,128)} fusion(f32[256,8,32]{0,2,1:T(8,128)S(1)} %bitcast.44, f32[256,8]{0,1:T(8,128)S(1)} %get-tuple-element.50, f32[8,32,128]{2,1,0:T(8,128)S(1)} %copy-done, f32[256,8]{0,1:T(8,128)S(1)} %get-tuple-element.49, f32[256,256]{1,0:T(8,128)S(1)} %get-tuple-element.47, f32[8]{0:T(128)S(1)} %exp.44), kind=kOutput, calls=%fused_computation.8 | convolution fusion | flops 16973824 | bytes 606720 | tf_op jit(solution)/shard_map/while/body/eval_jaxpr/sh,shp,sn->hpn/dot_general | solution.py:40
  78.4 1.6 %copy.28 = bf16[32,2048]{1,0:T(8,128)(2,1)} copy(bf16[32,2048]{1,0:T(8,128)(2,1)} %shard_map.159) | data formatting | bytes 262144
  (19 shorter events, 0.1 us)
Async XLA Ops:
  0.6 41.9 %copy-start.6 = (f32[4,256]{1,0:T(4,128)S(1)}, f32[4,256]{1,0:T(4,128)}, u32[]{:S(2)}) copy-start(f32[4,256]{1,0:T(4,128)} %param.21) | copy-start | bytes 12292
  0.6 41.9 %copy-start.3 = (f32[4,8,32]{2,1,0:T(8,128)S(1)}, f32[4,8,32]{2,1,0:T(8,128)}, u32[]{:S(2)}) copy-start(f32[4,8,32]{2,1,0:T(8,128)} %param.20) | copy-start | bytes 12292
  0.7 42.0 %copy-start.4 = (f32[3,8,32]{2,1,0:T(8,128)S(1)}, f32[3,8,32]{2,1,0:T(8,128)}, u32[]{:S(2)}) copy-start(f32[3,8,32]{2,1,0:T(8,128)} %param.22) | copy-start | bytes 9220
  0.7 42.3 %copy-start.5 = (f32[3,256]{1,0:T(4,128)S(1)}, f32[3,256]{1,0:T(4,128)}, u32[]{:S(2)}) copy-start(f32[3,256]{1,0:T(4,128)} %param.23) | copy-start | bytes 9220
  0.7 44.9 %copy-start.7 = (f32[8]{0:T(128)S(1)}, f32[8]{0:T(128)}, u32[]{:S(2)}) copy-start(f32[8]{0:T(128)} %param.24) | copy-start | bytes 100
  0.7 44.9 %copy-start.8 = (f32[8]{0:T(128)S(1)}, f32[8]{0:T(128)}, u32[]{:S(2)}) copy-start(f32[8]{0:T(128)} %param.25) | copy-start | bytes 100
  42.6 5.1 %copy-start.2 = (f32[8,256]{1,0:T(8,128)S(1)}, f32[8,256]{1,0:T(8,128)}, u32[]{:S(2)}) copy-start(f32[8,256]{1,0:T(8,128)} %get-tuple-element.25) | copy-start | bytes 24580
  45.1 3.2 %copy-start = (f32[8,32,128]{2,1,0:T(8,128)S(1)}, f32[8,32,128]{2,1,0:T(8,128)}, u32[]{:S(2)}) copy-start(f32[8,32,128]{2,1,0:T(8,128)} %param.27) | copy-start | bytes 393220
  47.6 1.1 %copy-start.9 = (f32[8]{0:T(128)S(1)}, f32[8]{0:T(128)}, u32[]{:S(2)}) copy-start(f32[8]{0:T(128)} %param.26) | copy-start | bytes 100
  47.7 1.1 %copy-start.1 = (f32[256,256]{1,0:T(8,128)S(1)}, f32[256,256]{1,0:T(8,128)}, u32[]{:S(2)}) copy-start(f32[256,256]{1,0:T(8,128)} %get-tuple-element.36) | copy-start | bytes 786436
